TPU v7x, 32 devices: a whole 2x2x4 slice. The times are simulated.
32 devices in a mesh: groups: 2 (over y), region: 4 (over z), slab: 2 (over x), chip: 2 (over core).
Axes of the slice: x: 2, y: 2, z: 4, core: 2. Of those that a mesh axis runs over, the one named last changes fastest.
Arguments:
- features: bfloat16 [16384, 256], P(('groups', 'region', 'slab', 'chip')), parts along dimension 0, may hold values from -6 to 6
- neighbours: int32 [27, 16384], P(None, ('groups', 'region', 'slab', 'chip')), parts along dimension 1, may hold values from -1 to 1279, as said below
- fetch_table: int32 [8, 2, 2, 4, 2], P('groups', 'slab', 'chip'), parts along dimension 0, may hold values from -1 to 7, as said below
- hilbert_slot: int32 [256], P(('groups', 'region', 'slab', 'chip')), parts along dimension 0, may hold values from 0 to 31, as said below
- patch_ids: int32 [16384], P(('groups', 'region', 'slab')), parts along dimension 0, may hold values from 0 to 7, never falling along the last dimension, each value on 1 to 2048 neighbouring positions
- conv_weight: bfloat16 [27, 256, 256], P(None, None, 'chip'), may hold values from -0.078125 to 0.078125
- cpe_weight: bfloat16 [256, 256], replicated, may hold values from -0.375 to 0.375
- cpe_bias: float32 [256], replicated, may hold values from -4 to 4
- cpe_gain: float32 [256], replicated, may hold values from 0.1 to 1.9
- cpe_shift: float32 [256], replicated, may hold values from -3 to 3
- norm1_gain: float32 [256], replicated, may hold values from 0.1 to 1.9
- norm1_shift: float32 [256], replicated, may hold values from -3 to 3
- query_weight: bfloat16 [256, 256], replicated, as said below
- pair_weight: bfloat16 [256, 512], replicated, as said below
- proj_weight: bfloat16 [256, 256], replicated, may hold values from -0.375 to 0.375
- norm2_gain: float32 [256], replicated, may hold values from 0.1 to 1.9
- norm2_shift: float32 [256], replicated, may hold values from -3 to 3
- fc1_weight: bfloat16 [256, 1024], replicated, may hold values from -0.375 to 0.375
- fc1_bias: float32 [1024], replicated, may hold values from -3 to 3
- fc2_weight: bfloat16 [1024, 256], replicated, may hold values from -0.1875 to 0.1875
Outputs:
- block_output: bfloat16 [16384, 256], P(('groups', 'region', 'slab', 'chip')), parts along dimension 0
There are 2 independent parts, one for each index of `groups`. A program takes and returns all parts, laid end to end along the dimension named above; an argument that names none is the same for every part. Nothing has to cross between parts.
Inputs may be any that keep to these rules, and one draw needn't show every extreme that they name: `neighbours`: indices into the device's pool; offset 27 // 2 is always the point itself, at pool index 128 plus its row on the device. `fetch_table`: block indices on the source device. `hilbert_slot`: for each slab and chip index, the values on the 4 devices of that index form a permutation of 0 .. 31; one device sends either exactly 4 blocks or none to each region. `query_weight`: real entries of magnitude at most 100 over the fan-in's square root. `pair_weight`: real entries of order 1 over the fan-in's square root.
All inputs are finite; a program needn't handle non-finite values.
Results may differ from a plain program's by a relative error of at most 0.012.
The roundings to bfloat16 on the way count: a program that leaves them out, or rounds other values in their place, can miss the bound.
Values may be sent and summed in bfloat16 or wider, within the bound.
A program may use at most 64 MiB of HBM per device.

v0:
```python
import math

import jax
import jax.numpy as jnp
from jax import lax
from jax.sharding import PartitionSpec as P

HEAD_DIM = 16
BLOCK = 64
HALO_B = 2


def with_halo(block, sides, width):
    for axis, dim in sides:
        count = lax.axis_size(axis)
        forward = [(i, i + 1) for i in range(count - 1)]
        backward = [(target, source) for source, target in forward]
        low = lax.ppermute(
            lax.slice_in_dim(block, block.shape[dim] - width, None, axis=dim), axis, forward
        )
        high = lax.ppermute(lax.slice_in_dim(block, 0, width, axis=dim), axis, backward)
        block = jnp.concatenate([low, block, high], axis=dim)
    return block


def layer_norm(values, gain, shift):
    mean = jnp.mean(values, axis=-1, keepdims=True)
    centered = values - mean
    var = jnp.mean(centered * centered, axis=-1, keepdims=True)
    return centered * lax.rsqrt(var + 1e-05) * gain + shift


def local(
    features,
    neighbours,
    fetch_table,
    hilbert_slot,
    patch_ids,
    conv_weight,
    cpe_weight,
    cpe_bias,
    cpe_gain,
    cpe_shift,
    norm1_gain,
    norm1_shift,
    query_weight,
    pair_weight,
    proj_weight,
    norm2_gain,
    norm2_shift,
    fc1_weight,
    fc1_bias,
    fc2_weight,
):
    rows_dev = features.shape[0]
    width = features.shape[1]
    count = rows_dev // BLOCK
    regions = lax.axis_size("region")
    blocks = features.reshape(count, BLOCK, width)
    framed = with_halo(blocks, (("slab", 0),), HALO_B)
    table = fetch_table[:, 0, 0]
    slots = table.shape[2]
    here = lax.axis_index("region")
    outgoing = lax.dynamic_index_in_dim(table, here, 0, keepdims=False)
    chosen = jnp.take(blocks, jnp.maximum(outgoing, 0).reshape(-1), axis=0).reshape(
        regions, slots, BLOCK, width
    )
    chosen = jnp.where((outgoing >= 0)[:, :, None, None], chosen, jnp.zeros_like(chosen))
    fetched = lax.all_to_all(chosen, "region", split_axis=0, concat_axis=0, tiled=True)
    pool = jnp.concatenate([framed.reshape(-1, width), fetched.reshape(-1, width)], axis=0)
    valid = neighbours >= 0
    rows = jnp.take(pool, jnp.where(valid, neighbours, 0), axis=0)
    rows = jnp.where(valid[..., None], rows, jnp.zeros_like(rows))
    conv = jnp.einsum(
        "kpc,kcd->pd",
        rows,
        lax.all_gather(conv_weight, "chip", axis=2, tiled=True),
        preferred_element_type=jnp.float32,
    ).astype(jnp.bfloat16)
    lin = jnp.dot(conv, cpe_weight, preferred_element_type=jnp.float32) + cpe_bias
    encoded = (features.astype(jnp.float32) + layer_norm(lin, cpe_gain, cpe_shift)).astype(
        jnp.bfloat16
    )
    cap = max(1, 2 * count // regions)
    region_of = hilbert_slot // count
    slot_of = hilbert_slot % count
    order = jnp.arange(count, dtype=jnp.int32)
    rank = jnp.sum(
        (region_of[:, None] == region_of[None, :]) & (order[:, None] > order[None, :]), axis=1
    )
    position = region_of * cap + rank
    pick = jnp.arange(regions * cap, dtype=jnp.int32)[:, None] == position[None, :]
    sending = jnp.dot(
        pick.astype(jnp.bfloat16),
        encoded.reshape(count, BLOCK * width),
        preferred_element_type=jnp.float32,
    ).astype(jnp.bfloat16)
    sending = sending.reshape(regions, cap, BLOCK * width)
    labels = (
        (jnp.sum(jnp.where(pick, slot_of[None, :] + 1, 0), axis=1) - 1)
        .astype(jnp.bfloat16)
        .reshape(regions, cap)
    )
    block_numbers = jnp.arange(count, dtype=jnp.int32).astype(jnp.bfloat16)
    arrived, marks = (
        lax.all_to_all(sending, "region", split_axis=0, concat_axis=0, tiled=True),
        lax.all_to_all(labels, "region", split_axis=0, concat_axis=0, tiled=True),
    )
    place_arrived = arrived.reshape(regions * cap, -1)
    place_marks = marks.reshape(-1)
    select = (place_marks[None, :] == block_numbers[:, None]).astype(jnp.bfloat16)
    reordered = (
        jnp.dot(select, place_arrived, preferred_element_type=jnp.float32)
        .astype(jnp.bfloat16)
        .reshape(rows_dev, width)
    )
    normed = layer_norm(reordered.astype(jnp.float32), norm1_gain, norm1_shift).astype(jnp.bfloat16)
    query_rows = jnp.dot(normed, query_weight, preferred_element_type=jnp.float32).astype(
        jnp.bfloat16
    )
    pair_rows = jnp.dot(normed, pair_weight, preferred_element_type=jnp.float32).astype(
        jnp.bfloat16
    )
    all_pairs = lax.all_gather(pair_rows, "chip", axis=0, tiled=True)
    key_count = all_pairs.shape[0]
    own_ids = lax.dynamic_slice_in_dim(patch_ids, lax.axis_index("chip") * rows_dev, rows_dev)
    same = own_ids[:, None] == patch_ids[None, :]
    heads = width // HEAD_DIM
    group = math.gcd(heads, 4)
    groups = heads // group
    scale = HEAD_DIM ** (-0.5)
    query_groups = query_rows.reshape(rows_dev, groups, group, HEAD_DIM).transpose(1, 0, 2, 3)
    key_groups = (
        all_pairs[:, :width].reshape(key_count, groups, group, HEAD_DIM).transpose(1, 0, 2, 3)
    )
    value_groups = (
        all_pairs[:, width:].reshape(key_count, groups, group, HEAD_DIM).transpose(1, 0, 2, 3)
    )

    def attend(parts):
        q_h, k_h, v_h = parts
        scores = jnp.einsum("qhd,khd->hqk", q_h, k_h, preferred_element_type=jnp.float32) * scale
        scores = jnp.where(same[None], scores, jnp.float32(-1e30))
        top = jnp.max(scores, axis=-1, keepdims=True)
        expo = jnp.exp(scores - top)
        weights = (expo / jnp.sum(expo, axis=-1, keepdims=True)).astype(jnp.bfloat16)
        return jnp.einsum("hqk,khd->qhd", weights, v_h, preferred_element_type=jnp.float32).astype(
            jnp.bfloat16
        )

    mixed = lax.map(attend, (query_groups, key_groups, value_groups))
    attended = mixed.transpose(1, 0, 2, 3).reshape(rows_dev, width)
    residual_mid = (
        reordered.astype(jnp.float32)
        + jnp.dot(attended, proj_weight, preferred_element_type=jnp.float32)
    ).astype(jnp.bfloat16)
    second_norm = layer_norm(residual_mid.astype(jnp.float32), norm2_gain, norm2_shift).astype(
        jnp.bfloat16
    )
    hidden = jax.nn.gelu(
        jnp.dot(second_norm, fc1_weight, preferred_element_type=jnp.float32) + fc1_bias,
        approximate=False,
    ).astype(jnp.bfloat16)
    return (
        residual_mid.astype(jnp.float32)
        + jnp.dot(hidden, fc2_weight, preferred_element_type=jnp.float32)
    ).astype(jnp.bfloat16)


def solution(mesh):
    return jax.shard_map(
        local,
        mesh=mesh,
        in_specs=(
            P(("groups", "region", "slab", "chip"), None),
            P(None, ("groups", "region", "slab", "chip")),
            P("groups", "slab", "chip", None, None),
            P(("groups", "region", "slab", "chip")),
            P(("groups", "region", "slab")),
            P(None, None, "chip"),
            P(),
            P(),
            P(),
            P(),
            P(),
            P(),
            P(),
            P(),
            P(),
            P(),
            P(),
            P(),
            P(),
            P(),
        ),
        out_specs=P(("groups", "region", "slab", "chip"), None),
        check_vma=False,
    )
```

profile of v0, /device:TPU:0, one launch (start us, length us, event | category | flops | bytes accessed | tf_op | source)
XLA Modules:
  0.0 166.7 jit_solution(46258074506811749)
XLA Ops:
  8.4 1.5 gather_fusion
  10.7 6.3 %all-to-all-start.1 = ((bf16[4,2,64,256]{3,2,1,0:T(8,128)(2,1)}), bf16[4,2,64,256]{3,2,1,0:T(8,128)(2,1)S(1)}, u32[]{:S(2)}, u32[]{:S(2)}) async-start(bf16[4,2,64,256]{3,2,1,0:T(8,128)(2,1)} %select_select_fusion), calls=%async_computation.1 | async-start | bytes 524288 | tf_op jit(solution)/shard_map/all_to_all | solution.py:69
  17.0 3.4 %collective-permute-start = (bf16[2,64,256]{2,1,0:T(8,128)(2,1)S(1)}, bf16[2,64,256]{2,1,0:T(8,128)(2,1)S(1)}, u32[]{:S(2)}, u32[]{:S(2)}) collective-permute-start(bf16[2,64,256]{2,1,0:T(8,128)(2,1)S(1)} %bitcast.99), channel_id=1, source_target_pairs={{0,2},{1,3},{4,6},{5,7},{8,10},{9,11},{12,14},{13,15},{16,18},{17,... | collective-permute-start | bytes 196616 | tf_op jit(solution)/shard_map/ppermute | solution.py:18
  20.4 1.3 collective-permute-start.1
  23.0 3.6 %collective-permute-done.1 = bf16[2,64,256]{2,1,0:T(8,128)(2,1)S(1)} collective-permute-done((bf16[2,64,256]{2,1,0:T(8,128)(2,1)S(1)}, bf16[2,64,256]{2,1,0:T(8,128)(2,1)S(1)}, u32[]{:S(2)}, u32[]{:S(2)}) %collective-permute-start.1) | collective-permute-done | bytes 65568 | tf_op jit(solution)/shard_map/ppermute | solution.py:21
  26.7 5.1 %all-to-all-start = ((bf16[4,1,4]{2,1,0:T(2,128)(2,1)}), bf16[4,1,4]{2,1,0:T(2,128)(2,1)S(1)}, u32[]{:S(2)}, u32[]{:S(2)}) async-start(bf16[4,1,4]{2,1,0:T(2,128)(2,1)} %convert_element_type.105), calls=%async_computation | async-start | bytes 4096 | tf_op jit(solution)/shard_map/all_to_all | solution.py:107
  31.8 38.7 %gather_fusion.1 = bf16[13824,256]{1,0:T(8,128)(2,1)} fusion(bf16[1280,256]{1,0:T(8,128)(2,1)S(1)} %pad_maximum_fusion, s32[14336]{0:T(1024)S(1)} %pad_clamp_fusion), kind=kCustom, calls=%fused_computation.1 | custom fusion | bytes 14211072 | tf_op jit(solution)/shard_map/jit(_take)/gather | solution.py:72
  70.6 9.4 %fusion.64.clone.1.clone.4 = bf16[512,256]{1,0:T(8,128)(2,1)S(1)} fusion(bf16[27,256,256]{2,1,0:T(8,128)(2,1)} %all-gather.3.cloned.1.call-done, bf16[27,512,256]{2,1,0:T(8,128)(2,1)} %bitcast.88, pred[27,512]{1,0:T(8,128)(4,1)S(1)} %get-tuple-element.79, pred[27,512]{1,0:T(8,128)(4,1)S(1)} %get-tuple-element.78), kind=kOutput, calls=%fused_computation.70.clone.clone.clone.clone.clone.1 | convolution fusion | flops 1819148288 | bytes 10906624 | tf_op jit(solution)/shard_map/kpc,kcd->pd/dot_general | solution.py:74
  81.4 1.0 reshape.162
  82.3 5.1 %all-to-all-start.2 = ((bf16[4,4,16384]{2,1,0:T(4,128)(2,1)}), bf16[4,4,16384]{2,1,0:T(4,128)(2,1)S(1)}, u32[]{:S(2)}, u32[]{:S(2)}) async-start(bf16[4,4,16384]{2,1,0:T(4,128)(2,1)} %reshape.162), calls=%async_computation.2 | async-start | bytes 1048576 | tf_op jit(solution)/shard_map/all_to_all | solution.py:106
  87.6 11.8 %all-to-all-done.2 = bf16[4,4,16384]{2,1,0:T(4,128)(2,1)S(1)} async-done(((bf16[4,4,16384]{2,1,0:T(4,128)(2,1)}), bf16[4,4,16384]{2,1,0:T(4,128)(2,1)S(1)}, u32[]{:S(2)}, u32[]{:S(2)}) %all-to-all-start.2) | async-done | bytes 524320 | tf_op jit(solution)/shard_map/all_to_all | solution.py:106
  100.3 1.2 convolution_convert_fusion.2
  102.3 6.6 %all-gather.5.cloned.1.call-done = bf16[1024,512]{1,0:T(8,128)(2,1)} async-done(((bf16[512,512]{1,0:T(8,128)(2,1)}), bf16[1024,512]{1,0:T(8,128)(2,1)}) %all-gather.5.cloned.1.call-update) | async-done | bytes 1048592 | tf_op jit(solution)/shard_map/all_gather | solution.py:124
  108.9 1.3 fusion.158
  110.6 41.5 %while.11 = (s32[]{:T(128)}, bf16[4,512,4,16]{1,3,2,0:T(8,128)(2,1)S(1)}, bf16[4,1024,4,16]{1,3,2,0:T(8,128)(2,1)S(1)}, bf16[4,512,4,16]{1,3,2,0:T(8,128)(2,1)S(...) while((s32[]{:T(128)}, ...), condition=%wide.region_9.10_spmd.clone, body=%wide.region_6.9_spmd.clone.sunk | while | flops 147358720 | bytes 18243668 | solution.py:151
  111.0 5.4 %fusion.190 = (f32[4,512]{1,0:T(4,128)S(1)}, f32[4,512,1024]{2,1,0:T(8,128)}) fusion(pred[512,1024]{1,0:T(8,128)(4,1)S(1)} %broadcast_compare_fusion.4, bf16[4,1024,4,16]{1,3,2,0:T(8,128)(2,1)S(1)} %get-tuple-element.154, s32[]{:T(128)} %get-tuple-element.142, bf16[4,512,4,16]{1,3,2,0:T(8,128)(2,1)S(1)} %get-tuple-element.153), kind=kOutput, calls=%fused_computation.180.clone.1 | convolution fusion | flops 75498496 | bytes 9118720 | tf_op jit(solution)/shard_map/while/body/eval_jaxpr/sub | solution.py:145
  116.4 4.6 %fusion.191 = bf16[4,512,4,16]{1,3,2,0:T(8,128)(2,1)S(1)} fusion(bf16[4,512,4,16]{1,3,2,0:T(8,128)(2,1)S(1)} %get-tuple-element.143, s32[]{:T(128)} %get-tuple-element.142, f32[4,512,1024]{2,1,0:T(8,128)} %get-tuple-element.132, f32[4,512]{1,0:T(4,128)S(1)} %get-tuple-element.133, bf16[4,1024,4,16]{1,3,2,0:T(8,128)(2,1)S(1)} %get-tuple-element.152), kind=kOutput, calls=%fused_computation.14.clone.1 | convolution fusion | flops 71335936 | bytes 8594432 | tf_op jit(solution)/shard_map/while/body/eval_jaxpr/hqk,khd->qhd/dot_general | solution.py:147
  121.4 5.4 %fusion.190 = (f32[4,512]{1,0:T(4,128)S(1)}, f32[4,512,1024]{2,1,0:T(8,128)}) fusion(pred[512,1024]{1,0:T(8,128)(4,1)S(1)} %broadcast_compare_fusion.4, bf16[4,1024,4,16]{1,3,2,0:T(8,128)(2,1)S(1)} %get-tuple-element.154, s32[]{:T(128)} %get-tuple-element.142, bf16[4,512,4,16]{1,3,2,0:T(8,128)(2,1)S(1)} %get-tuple-element.153), kind=kOutput, calls=%fused_computation.180.clone.1 | convolution fusion | flops 75498496 | bytes 9118720 | tf_op jit(solution)/shard_map/while/body/eval_jaxpr/sub | solution.py:145
  126.8 4.6 %fusion.191 = bf16[4,512,4,16]{1,3,2,0:T(8,128)(2,1)S(1)} fusion(bf16[4,512,4,16]{1,3,2,0:T(8,128)(2,1)S(1)} %get-tuple-element.143, s32[]{:T(128)} %get-tuple-element.142, f32[4,512,1024]{2,1,0:T(8,128)} %get-tuple-element.132, f32[4,512]{1,0:T(4,128)S(1)} %get-tuple-element.133, bf16[4,1024,4,16]{1,3,2,0:T(8,128)(2,1)S(1)} %get-tuple-element.152), kind=kOutput, calls=%fused_computation.14.clone.1 | convolution fusion | flops 71335936 | bytes 8594432 | tf_op jit(solution)/shard_map/while/body/eval_jaxpr/hqk,khd->qhd/dot_general | solution.py:147
  131.8 5.4 %fusion.190 = (f32[4,512]{1,0:T(4,128)S(1)}, f32[4,512,1024]{2,1,0:T(8,128)}) fusion(pred[512,1024]{1,0:T(8,128)(4,1)S(1)} %broadcast_compare_fusion.4, bf16[4,1024,4,16]{1,3,2,0:T(8,128)(2,1)S(1)} %get-tuple-element.154, s32[]{:T(128)} %get-tuple-element.142, bf16[4,512,4,16]{1,3,2,0:T(8,128)(2,1)S(1)} %get-tuple-element.153), kind=kOutput, calls=%fused_computation.180.clone.1 | convolution fusion | flops 75498496 | bytes 9118720 | tf_op jit(solution)/shard_map/while/body/eval_jaxpr/sub | solution.py:145
  137.1 4.6 %fusion.191 = bf16[4,512,4,16]{1,3,2,0:T(8,128)(2,1)S(1)} fusion(bf16[4,512,4,16]{1,3,2,0:T(8,128)(2,1)S(1)} %get-tuple-element.143, s32[]{:T(128)} %get-tuple-element.142, f32[4,512,1024]{2,1,0:T(8,128)} %get-tuple-element.132, f32[4,512]{1,0:T(4,128)S(1)} %get-tuple-element.133, bf16[4,1024,4,16]{1,3,2,0:T(8,128)(2,1)S(1)} %get-tuple-element.152), kind=kOutput, calls=%fused_computation.14.clone.1 | convolution fusion | flops 71335936 | bytes 8594432 | tf_op jit(solution)/shard_map/while/body/eval_jaxpr/hqk,khd->qhd/dot_general | solution.py:147
  142.2 5.4 %fusion.190 = (f32[4,512]{1,0:T(4,128)S(1)}, f32[4,512,1024]{2,1,0:T(8,128)}) fusion(pred[512,1024]{1,0:T(8,128)(4,1)S(1)} %broadcast_compare_fusion.4, bf16[4,1024,4,16]{1,3,2,0:T(8,128)(2,1)S(1)} %get-tuple-element.154, s32[]{:T(128)} %get-tuple-element.142, bf16[4,512,4,16]{1,3,2,0:T(8,128)(2,1)S(1)} %get-tuple-element.153), kind=kOutput, calls=%fused_computation.180.clone.1 | convolution fusion | flops 75498496 | bytes 9118720 | tf_op jit(solution)/shard_map/while/body/eval_jaxpr/sub | solution.py:145
  147.5 4.6 %fusion.191 = bf16[4,512,4,16]{1,3,2,0:T(8,128)(2,1)S(1)} fusion(bf16[4,512,4,16]{1,3,2,0:T(8,128)(2,1)S(1)} %get-tuple-element.143, s32[]{:T(128)} %get-tuple-element.142, f32[4,512,1024]{2,1,0:T(8,128)} %get-tuple-element.132, f32[4,512]{1,0:T(4,128)S(1)} %get-tuple-element.133, bf16[4,1024,4,16]{1,3,2,0:T(8,128)(2,1)S(1)} %get-tuple-element.152), kind=kOutput, calls=%fused_computation.14.clone.1 | convolution fusion | flops 71335936 | bytes 8594432 | tf_op jit(solution)/shard_map/while/body/eval_jaxpr/hqk,khd->qhd/dot_general | solution.py:147
  152.6 6.4 %fusion.67 = bf16[512,256]{0,1:T(8,128)(2,1)S(1)} fusion(f32[512,256]{0,1:T(8,128)S(1)} %get-tuple-element.86, bf16[1024,256]{1,0:T(8,128)(2,1)S(1)} %copy-done, bf16[256,1024]{1,0:T(8,128)(2,1)} %param.39, f32[1024]{0:T(1024)S(1)} %copy-done.13, f32[256]{0:T(256)S(1)} %copy-done.14, f32[256]{0:T(256)S(1)} %copy-done.15, f32[512]{0:T(512)S(1)} %add_rsqrt_fusion, ...), kind=kOutput, calls=%fused_computation.71 | convolution fusion | flops 572391424 | bytes 1845248 | tf_op jit(solution)/shard_map/dot_general | solution.py:166
  (96 shorter events, 10.1 us)
Async XLA Ops:
  6.5 146.1 %copy-start = (bf16[1024,256]{1,0:T(8,128)(2,1)S(1)}, bf16[1024,256]{1,0:T(8,128)(2,1)}, u32[]{:S(2)}) copy-start(bf16[1024,256]{1,0:T(8,128)(2,1)} %param.41) | copy-start | bytes 1572868
  6.5 10.5 %copy-start.1 = (bf16[512,256]{1,0:T(8,128)(2,1)S(1)}, bf16[512,256]{1,0:T(8,128)(2,1)}, u32[]{:S(2)}) copy-start(bf16[512,256]{1,0:T(8,128)(2,1)} %param.22) | copy-start | bytes 786436
  6.5 15.2 %copy-start.3 = (s32[27,512]{1,0:T(8,128)S(1)}, s32[27,512]{1,0:T(8,128)}, u32[]{:S(2)}) copy-start(s32[27,512]{1,0:T(8,128)} %param.23) | copy-start | bytes 165892
  6.5 15.2 %copy-start.16 = (s32[8]{0:T(128)S(1)}, s32[8]{0:T(128)}, u32[]{:S(2)}) copy-start(s32[8]{0:T(128)} %param.25) | copy-start | bytes 100
  6.5 64.0 %all-gather.3.cloned.1.call-start = ((), (), s32[]{:S(2)}) async-start(), calls=%async_computation.3 | async-start | bytes 5308416 | tf_op jit(solution)/shard_map/all_gather | solution.py:77
  10.7 16.0 %all-to-all-start.1 = ((bf16[4,2,64,256]{3,2,1,0:T(8,128)(2,1)}), bf16[4,2,64,256]{3,2,1,0:T(8,128)(2,1)S(1)}, u32[]{:S(2)}, u32[]{:S(2)}) async-start(bf16[4,2,64,256]{3,2,1,0:T(8,128)(2,1)} %select_select_fusion), calls=%async_computation.1 | async-start | bytes 524288 | tf_op jit(solution)/shard_map/all_to_all | solution.py:69
  17.0 5.9 %collective-permute-start = (bf16[2,64,256]{2,1,0:T(8,128)(2,1)S(1)}, bf16[2,64,256]{2,1,0:T(8,128)(2,1)S(1)}, u32[]{:S(2)}, u32[]{:S(2)}) collective-permute-start(bf16[2,64,256]{2,1,0:T(8,128)(2,1)S(1)} %bitcast.99), channel_id=1, source_target_pairs={{0,2},{1,3},{4,6},{5,7},{8,10},{9,11},{12,14},{13,15},{16,18},{17,... | collective-permute-start | bytes 196616 | tf_op jit(solution)/shard_map/ppermute | solution.py:18
  20.4 6.2 %collective-permute-start.1 = (bf16[2,64,256]{2,1,0:T(8,128)(2,1)S(1)}, bf16[2,64,256]{2,1,0:T(8,128)(2,1)S(1)}, u32[]{:S(2)}, u32[]{:S(2)}) collective-permute-start(bf16[2,64,256]{2,1,0:T(8,128)(2,1)S(1)} %bitcast.98), channel_id=1, source_target_pairs={{2,0},{3,1},{6,4},{7,5},{10,8},{11,9},{14,12},{15,13},{18,16},{19,... | collective-permute-start | bytes 196616 | tf_op jit(solution)/shard_map/ppermute | solution.py:21
  26.7 55.7 %all-to-all-start = ((bf16[4,1,4]{2,1,0:T(2,128)(2,1)}), bf16[4,1,4]{2,1,0:T(2,128)(2,1)S(1)}, u32[]{:S(2)}, u32[]{:S(2)}) async-start(bf16[4,1,4]{2,1,0:T(2,128)(2,1)} %convert_element_type.105), calls=%async_computation | async-start | bytes 4096 | tf_op jit(solution)/shard_map/all_to_all | solution.py:107
  70.6 9.5 %copy-start.5 = (bf16[256,256]{1,0:T(8,128)(2,1)S(1)}, bf16[256,256]{1,0:T(8,128)(2,1)}, u32[]{:S(2)}) copy-start(bf16[256,256]{1,0:T(8,128)(2,1)} %param.28) | copy-start | bytes 393220
  70.6 9.5 %copy-start.10 = (f32[256]{0:T(256)S(1)}, f32[256]{0:T(256)}, u32[]{:S(2)}) copy-start(f32[256]{0:T(256)} %param.29) | copy-start | bytes 3076
  70.6 9.9 %copy-start.11 = (f32[256]{0:T(256)S(1)}, f32[256]{0:T(256)}, u32[]{:S(2)}) copy-start(f32[256]{0:T(256)} %param.31) | copy-start | bytes 3076
  70.6 9.9 %copy-start.12 = (f32[256]{0:T(256)S(1)}, f32[256]{0:T(256)}, u32[]{:S(2)}) copy-start(f32[256]{0:T(256)} %param.30) | copy-start | bytes 3076
  82.3 17.0 %all-to-all-start.2 = ((bf16[4,4,16384]{2,1,0:T(4,128)(2,1)}), bf16[4,4,16384]{2,1,0:T(4,128)(2,1)S(1)}, u32[]{:S(2)}, u32[]{:S(2)}) async-start(bf16[4,4,16384]{2,1,0:T(4,128)(2,1)} %reshape.162), calls=%async_computation.2 | async-start | bytes 1048576 | tf_op jit(solution)/shard_map/all_to_all | solution.py:106
  87.4 21.5 %all-gather.5.cloned.1.call-start = ((), (), s32[]{:S(2)}) async-start(), calls=%async_computation.4 | async-start | bytes 1572864 | tf_op jit(solution)/shard_map/all_gather | solution.py:124
  87.6 12.8 %copy-start.2 = (bf16[256,512]{1,0:T(8,128)(2,1)S(1)}, bf16[256,512]{1,0:T(8,128)(2,1)}, u32[]{:S(2)}) copy-start(bf16[256,512]{1,0:T(8,128)(2,1)} %param.35) | copy-start | bytes 786436
  87.6 12.8 %copy-start.8 = (f32[256]{0:T(256)S(1)}, f32[256]{0:T(256)}, u32[]{:S(2)}) copy-start(f32[256]{0:T(256)} %param.33) | copy-start | bytes 3076
  87.6 12.8 %copy-start.9 = (f32[256]{0:T(256)S(1)}, f32[256]{0:T(256)}, u32[]{:S(2)}) copy-start(f32[256]{0:T(256)} %param.32) | copy-start | bytes 3076
  99.8 1.8 %copy-start.7 = (s32[1024]{0:T(1024)S(1)}, s32[1024]{0:T(1024)}, u32[]{:S(2)}) copy-start(s32[1024]{0:T(1024)} %param.26) | copy-start | bytes 12292
  99.9 1.9 %copy-start.4 = (bf16[256,256]{1,0:T(8,128)(2,1)S(1)}, bf16[256,256]{1,0:T(8,128)(2,1)}, u32[]{:S(2)}) copy-start(bf16[256,256]{1,0:T(8,128)(2,1)} %param.34) | copy-start | bytes 393220
  110.6 41.6 %copy-start.6 = (bf16[256,256]{1,0:T(8,128)(2,1)S(1)}, bf16[256,256]{1,0:T(8,128)(2,1)}, u32[]{:S(2)}) copy-start(bf16[256,256]{1,0:T(8,128)(2,1)} %param.36) | copy-start | bytes 393220
  110.6 42.0 %copy-start.13 = (f32[1024]{0:T(1024)S(1)}, f32[1024]{0:T(1024)}, u32[]{:S(2)}) copy-start(f32[1024]{0:T(1024)} %param.40) | copy-start | bytes 12292
  110.6 42.0 %copy-start.14 = (f32[256]{0:T(256)S(1)}, f32[256]{0:T(256)}, u32[]{:S(2)}) copy-start(f32[256]{0:T(256)} %param.38) | copy-start | bytes 3076
  110.6 42.0 %copy-start.15 = (f32[256]{0:T(256)S(1)}, f32[256]{0:T(256)}, u32[]{:S(2)}) copy-start(f32[256]{0:T(256)} %param.37) | copy-start | bytes 3076
Sparse Core Ops, SparseCore 0:
  8.9 14.8 all-gather.2
  101.6 7.2 all-gather.4
where the time goes:
time: 168 us; the launch traced here: 167 us
  matrix products  58.7 us (35%)
  local copies, waits for them, and re-layouts  45.9 us (27%)
  waiting for transfers between devices  22.8 us (14%)
  starting transfers between devices  21.2 us (13%)
  between operations  13.8 us (8%)
  other arithmetic  4.25 us (3%)
    gather x1, local copies, waits for them, and re-layouts, local(): rows = jnp.take(pool, jnp.where(valid, neighbours, 0), axis=0)  38.7 us
    sub x4, matrix products, attend(): expo = jnp.exp(scores - top)  21.4 us
    dot_general x4, matrix products, attend(): jnp.einsum('hqk,khd->qhd', weights, v_h, preferred_element_type=jnp.float32)  18.6 us
    all_to_all x1, waiting for transfers between devices, local(): lax.all_to_all(sending, 'region', split_axis=0, concat_axis=0, tiled=True)  11.8 us
    dot_general x1, matrix products, local(): jnp.einsum('kpc,kcd->pd', rows, lax.all_gather(conv_weight, 'chip', axis=...  9.43 us
    all_gather x1, waiting for transfers between devices, local(): all_pairs = lax.all_gather(pair_rows, 'chip', axis=0, tiled=True)  6.64 us
    dot_general x1, matrix products, local(): jnp.dot(hidden, fc2_weight, preferred_element_type=jnp.float32)  6.43 us
    all_to_all x1, starting transfers between devices, local(): lax.all_to_all(chosen, 'region', split_axis=0, concat_axis=0, tiled=True)  6.32 us
  transfers between devices with their start and end apart: 7, of which 3 were waited for; matrix products, arithmetic and copies ran while one was open for 34% of the time, Pallas kernels for 0%

commit v1 on v0

--- a/solution.py
+++ b/solution.py
@@ -1,13 +1,17 @@
-import math
+import functools
 
 import jax
 import jax.numpy as jnp
 from jax import lax
+from jax.experimental import pallas as pl
+from jax.experimental.pallas import tpu as pltpu
 from jax.sharding import PartitionSpec as P
 
 HEAD_DIM = 16
 BLOCK = 64
 HALO_B = 2
+LANES = 128
+VMEM_BYTES = 48 * 1024 * 1024
 
 
 def with_halo(block, sides, width):
@@ -28,6 +32,126 @@
     centered = values - mean
     var = jnp.mean(centered * centered, axis=-1, keepdims=True)
     return centered * lax.rsqrt(var + 1e-05) * gain + shift
+
+
+def dot32(a, b):
+    return jnp.dot(a, b, preferred_element_type=jnp.float32)
+
+
+def conv_kernel(
+    nbr_ref, pool_ref, weight_ref, feat_ref, lin_ref, bias_ref, gain_ref, shift_ref,
+    out_ref, codes, marks, acc,
+):
+    offsets = weight_ref.shape[0]
+    rows = feat_ref.shape[0]
+    tiles = pool_ref.shape[0] // LANES
+    numbers = nbr_ref[...].T
+    low = jnp.bitwise_and(numbers, LANES - 1) + LANES
+    high = jnp.right_shift(jnp.maximum(numbers, 0), 7)
+    coded = jnp.where(numbers >= 0, jnp.left_shift(low, high), 0).astype(jnp.float32)
+    for o in range(offsets):
+        codes[o] = jnp.broadcast_to(coded[:, o : o + 1], (rows, LANES)).astype(jnp.bfloat16)
+    lane = lax.broadcasted_iota(jnp.int32, (16, LANES), 1) + LANES
+    for t in range(tiles):
+        marks[t] = jnp.left_shift(lane, t).astype(jnp.float32).astype(jnp.bfloat16)
+    acc[...] = jnp.zeros_like(acc)
+    one = jnp.ones((rows, LANES), jnp.bfloat16)
+    zero = jnp.zeros((rows, LANES), jnp.bfloat16)
+
+    def step(o, carry):
+        code = codes[o]
+        pick = jnp.concatenate(
+            [
+                jnp.where(code == jnp.tile(marks[t], (rows // 16, 1)), one, zero)
+                for t in range(tiles)
+            ],
+            axis=1,
+        )
+        got = dot32(pick, pool_ref[...]).astype(jnp.bfloat16)
+        acc[...] += dot32(got, weight_ref[o])
+        return carry
+
+    lax.fori_loop(0, offsets, step, 0)
+    conv = acc[...].astype(jnp.bfloat16)
+    lin = dot32(conv, lin_ref[...]) + bias_ref[...]
+    out_ref[...] = (
+        feat_ref[...].astype(jnp.float32) + layer_norm(lin, gain_ref[...], shift_ref[...])
+    ).astype(jnp.bfloat16)
+
+
+def conv_call(neighbours, pool, weight, features, lin, bias, gain, shift):
+    rows, width = features.shape
+    offsets = weight.shape[0]
+    tiles = pool.shape[0] // LANES
+    return pl.pallas_call(
+        conv_kernel,
+        out_shape=jax.ShapeDtypeStruct((rows, width), jnp.bfloat16),
+        in_specs=[pl.BlockSpec(memory_space=pltpu.VMEM)] * 8,
+        out_specs=pl.BlockSpec(memory_space=pltpu.VMEM),
+        scratch_shapes=[
+            pltpu.VMEM((offsets, rows, LANES), jnp.bfloat16),
+            pltpu.VMEM((tiles, 16, LANES), jnp.bfloat16),
+            pltpu.VMEM((rows, width), jnp.float32),
+        ],
+        compiler_params=pltpu.CompilerParams(vmem_limit_bytes=VMEM_BYTES),
+        name="conv",
+    )(neighbours, pool, weight, features, lin, bias[None], gain[None], shift[None])
+
+
+def tail_kernel(
+    rows_ref, query_ref, pairs_ref, own_ref, ids_ref, proj_ref, gain_ref, shift_ref,
+    fc1_ref, fc1_bias_ref, fc2_ref, out_ref, bias, mixed, part,
+):
+    rows, width = rows_ref.shape
+    heads = width // HEAD_DIM
+    bias[...] = jnp.where(own_ref[...] == ids_ref[...], 0.0, -1e30)
+    mixed[...] = jnp.zeros_like(mixed)
+    lane = lax.broadcasted_iota(jnp.int32, (1, width), 1) // HEAD_DIM
+
+    def head(h, carry):
+        mine = lane == h
+        query = jnp.where(mine, query_ref[...], jnp.zeros((), jnp.bfloat16))
+        values = jnp.where(mine, pairs_ref[:, width:], jnp.zeros((), jnp.bfloat16))
+        keys = pairs_ref[:, :width]
+        for r in range(0, rows, part):
+            scores = lax.dot_general(
+                query[r : r + part], keys, (((1,), (1,)), ((), ())),
+                preferred_element_type=jnp.float32,
+            ) + bias[r : r + part]
+            top = jnp.max(scores, axis=-1, keepdims=True)
+            expo = jnp.exp(scores - top)
+            total = jnp.sum(expo, axis=-1, keepdims=True)
+            weights = (expo * (1.0 / total)).astype(jnp.bfloat16)
+            mixed[r : r + part] += dot32(weights, values)
+        return carry
+
+    lax.fori_loop(0, heads, head, 0)
+    attended = mixed[...].astype(jnp.bfloat16)
+    mid = (rows_ref[...].astype(jnp.float32) + dot32(attended, proj_ref[...])).astype(jnp.bfloat16)
+    mid32 = mid.astype(jnp.float32)
+    normed = layer_norm(mid32, gain_ref[...], shift_ref[...]).astype(jnp.bfloat16)
+    pre = dot32(normed, fc1_ref[...]) + fc1_bias_ref[...]
+    hidden = (0.5 * pre * (1.0 + lax.erf(pre * (0.5**0.5)))).astype(jnp.bfloat16)
+    out_ref[...] = (mid32 + dot32(hidden, fc2_ref[...])).astype(jnp.bfloat16)
+
+
+def tail_call(reordered, queries, pairs, own_ids, ids, proj, gain, shift, fc1, fc1_bias, fc2):
+    rows, width = reordered.shape
+    return pl.pallas_call(
+        functools.partial(tail_kernel, part=128),
+        out_shape=jax.ShapeDtypeStruct((rows, width), jnp.bfloat16),
+        in_specs=[pl.BlockSpec(memory_space=pltpu.VMEM)] * 11,
+        out_specs=pl.BlockSpec(memory_space=pltpu.VMEM),
+        scratch_shapes=[
+            pltpu.VMEM((rows, pairs.shape[0]), jnp.float32),
+            pltpu.VMEM((rows, width), jnp.float32),
+        ],
+        compiler_params=pltpu.CompilerParams(vmem_limit_bytes=VMEM_BYTES),
+        name="tail",
+    )(
+        reordered, queries, pairs, own_ids[:, None], ids[None], proj, gain[None], shift[None],
+        fc1, fc1_bias[None], fc2,
+    )
 
 
 def local(
@@ -68,18 +192,9 @@
     chosen = jnp.where((outgoing >= 0)[:, :, None, None], chosen, jnp.zeros_like(chosen))
     fetched = lax.all_to_all(chosen, "region", split_axis=0, concat_axis=0, tiled=True)
     pool = jnp.concatenate([framed.reshape(-1, width), fetched.reshape(-1, width)], axis=0)
-    valid = neighbours >= 0
-    rows = jnp.take(pool, jnp.where(valid, neighbours, 0), axis=0)
-    rows = jnp.where(valid[..., None], rows, jnp.zeros_like(rows))
-    conv = jnp.einsum(
-        "kpc,kcd->pd",
-        rows,
-        lax.all_gather(conv_weight, "chip", axis=2, tiled=True),
-        preferred_element_type=jnp.float32,
-    ).astype(jnp.bfloat16)
-    lin = jnp.dot(conv, cpe_weight, preferred_element_type=jnp.float32) + cpe_bias
-    encoded = (features.astype(jnp.float32) + layer_norm(lin, cpe_gain, cpe_shift)).astype(
-        jnp.bfloat16
+    weight = lax.all_gather(conv_weight, "chip", axis=2, tiled=True)
+    encoded = conv_call(
+        neighbours, pool, weight, features, cpe_weight, cpe_bias, cpe_gain, cpe_shift
     )
     cap = max(1, 2 * count // regions)
     region_of = hilbert_slot // count
@@ -117,54 +232,16 @@
     normed = layer_norm(reordered.astype(jnp.float32), norm1_gain, norm1_shift).astype(jnp.bfloat16)
     query_rows = jnp.dot(normed, query_weight, preferred_element_type=jnp.float32).astype(
         jnp.bfloat16
-    )
+    ) * jnp.bfloat16(HEAD_DIM ** (-0.5))
     pair_rows = jnp.dot(normed, pair_weight, preferred_element_type=jnp.float32).astype(
         jnp.bfloat16
     )
     all_pairs = lax.all_gather(pair_rows, "chip", axis=0, tiled=True)
-    key_count = all_pairs.shape[0]
     own_ids = lax.dynamic_slice_in_dim(patch_ids, lax.axis_index("chip") * rows_dev, rows_dev)
-    same = own_ids[:, None] == patch_ids[None, :]
-    heads = width // HEAD_DIM
-    group = math.gcd(heads, 4)
-    groups = heads // group
-    scale = HEAD_DIM ** (-0.5)
-    query_groups = query_rows.reshape(rows_dev, groups, group, HEAD_DIM).transpose(1, 0, 2, 3)
-    key_groups = (
-        all_pairs[:, :width].reshape(key_count, groups, group, HEAD_DIM).transpose(1, 0, 2, 3)
-    )
-    value_groups = (
-        all_pairs[:, width:].reshape(key_count, groups, group, HEAD_DIM).transpose(1, 0, 2, 3)
-    )
-
-    def attend(parts):
-        q_h, k_h, v_h = parts
-        scores = jnp.einsum("qhd,khd->hqk", q_h, k_h, preferred_element_type=jnp.float32) * scale
-        scores = jnp.where(same[None], scores, jnp.float32(-1e30))
-        top = jnp.max(scores, axis=-1, keepdims=True)
-        expo = jnp.exp(scores - top)
-        weights = (expo / jnp.sum(expo, axis=-1, keepdims=True)).astype(jnp.bfloat16)
-        return jnp.einsum("hqk,khd->qhd", weights, v_h, preferred_element_type=jnp.float32).astype(
-            jnp.bfloat16
-        )
-
-    mixed = lax.map(attend, (query_groups, key_groups, value_groups))
-    attended = mixed.transpose(1, 0, 2, 3).reshape(rows_dev, width)
-    residual_mid = (
-        reordered.astype(jnp.float32)
-        + jnp.dot(attended, proj_weight, preferred_element_type=jnp.float32)
-    ).astype(jnp.bfloat16)
-    second_norm = layer_norm(residual_mid.astype(jnp.float32), norm2_gain, norm2_shift).astype(
-        jnp.bfloat16
-    )
-    hidden = jax.nn.gelu(
-        jnp.dot(second_norm, fc1_weight, preferred_element_type=jnp.float32) + fc1_bias,
-        approximate=False,
-    ).astype(jnp.bfloat16)
-    return (
-        residual_mid.astype(jnp.float32)
-        + jnp.dot(hidden, fc2_weight, preferred_element_type=jnp.float32)
-    ).astype(jnp.bfloat16)
+    return tail_call(
+        reordered, query_rows, all_pairs, own_ids, patch_ids, proj_weight, norm2_gain,
+        norm2_shift, fc1_weight, fc1_bias, fc2_weight,
+    )
 
 
 def solution(mesh):

time: 168 us -> 130 us (0.77)
  Pallas kernels: 0 us -> 60 us
  matrix products: 58.7 us -> 2.16 us
  local copies, waits for them, and re-layouts: 45.9 us -> 6.64 us
  other arithmetic: 4.25 us -> 2.31 us
    pallas_call x0 -> x2, Pallas kernels: none -> 60 us  [the longest x1 39.4 us: tail_call(): pl.pallas_call(functools.partial(tail_kernel, part=128), out_shape=jax.Sh...]
    gather x1 -> x0, local copies, waits for them, and re-layouts: 38.7 us -> none  [local(): rows = jnp.take(pool, jnp.where(valid, neighbours, 0), axis=0)]
    dot_general x8 -> x0, matrix products: 35 us -> none  [the longest x4 18.6 us: attend(): jnp.einsum('hqk,khd->qhd', weights, v_h, preferred_element_type=jnp.float32)]
    sub x4 -> x0, matrix products: 21.4 us -> none  [attend(): expo = jnp.exp(scores - top)]
    unnamed x35 -> x40, local copies, waits for them, and re-layouts: 0.22 us -> 3.31 us
    slice x3 -> x0, local copies, waits for them, and re-layouts: 1.68 us -> none  [the longest x2 1.47 us: local(): all_pairs[:, :width].reshape(key_count, groups, group, HEAD_DIM)]
  transfers between devices with their start and end apart: 7 -> 7, of which waited for: 3 -> 3; matrix products, arithmetic and copies ran while one was open for 34% -> 4% of each run, Pallas kernels for 0% -> 16%
where the time goes in v1:
time: 130 us; the launch traced here: 129 us
  Pallas kernels  60 us (46%)
  waiting for transfers between devices  23.2 us (18%)
  starting transfers between devices  21.3 us (16%)
  between operations  13.8 us (11%)
  local copies, waits for them, and re-layouts  6.64 us (5%)
  other arithmetic  2.31 us (2%)
  matrix products  2.16 us (2%)
    pallas_call x1, Pallas kernels, tail_call(): pl.pallas_call(functools.partial(tail_kernel, part=128), out_shape=jax.Sh...  39.4 us
    pallas_call x1, Pallas kernels, conv_call(): pl.pallas_call(conv_kernel, out_shape=jax.ShapeDtypeStruct((rows, width),...  20.6 us
    all_to_all x1, waiting for transfers between devices, local(): lax.all_to_all(sending, 'region', split_axis=0, concat_axis=0, tiled=True)  11.8 us
    all_gather x1, waiting for transfers between devices, local(): all_pairs = lax.all_gather(pair_rows, 'chip', axis=0, tiled=True)  6.79 us
    all_to_all x1, starting transfers between devices, local(): lax.all_to_all(chosen, 'region', split_axis=0, concat_axis=0, tiled=True)  6.32 us
    all_to_all x1, starting transfers between devices, local(): lax.all_to_all(labels, 'region', split_axis=0, concat_axis=0, tiled=True)  5.1 us
    all_to_all x1, starting transfers between devices, local(): lax.all_to_all(sending, 'region', split_axis=0, concat_axis=0, tiled=True)  5.09 us
    ppermute x1, waiting for transfers between devices, with_halo(): lax.ppermute(lax.slice_in_dim(block, 0, width, axis=dim), axis, backward)  3.86 us
  transfers between devices with their start and end apart: 7, of which 3 were waited for; matrix products, arithmetic and copies ran while one was open for 4% of the time, Pallas kernels for 16%

profile of v1, /device:TPU:0, one launch (start us, length us, event | category | flops | bytes accessed | tf_op | source)
XLA Modules:
  0.0 129.4 jit_solution(17296774865947048145)
XLA Ops:
  6.5 0.7 all-gather.3.cloned.1.call-update
  7.3 0.7 broadcast_compare_fusion
  8.4 0.6 gather_fusion
  8.9 0.8 select_select_fusion
  9.7 6.3 %all-to-all-start.1 = ((bf16[4,2,64,256]{3,2,1,0:T(8,128)(2,1)}), bf16[4,2,64,256]{3,2,1,0:T(8,128)(2,1)S(1)}, u32[]{:S(2)}, u32[]{:S(2)}) async-start(bf16[4,2,64,256]{3,2,1,0:T(8,128)(2,1)} %select_select_fusion), calls=%async_computation.1 | async-start | bytes 524288 | tf_op jit(solution)/shard_map/all_to_all | solution.py:193
  16.1 3.5 %collective-permute-start = (bf16[2,64,256]{2,1,0:T(8,128)(2,1)S(1)}, bf16[2,64,256]{2,1,0:T(8,128)(2,1)S(1)}, u32[]{:S(2)}, u32[]{:S(2)}) collective-permute-start(bf16[2,64,256]{2,1,0:T(8,128)(2,1)S(1)} %bitcast.33), channel_id=1, source_target_pairs={{0,2},{1,3},{4,6},{5,7},{8,10},{9,11},{12,14},{13,15},{16,18},{17,... | collective-permute-start | bytes 196616 | tf_op jit(solution)/shard_map/ppermute | solution.py:22
  19.7 1.3 collective-permute-start.1
  21.0 0.2 convert_reduce_fusion.1
  21.3 0.7 convert_element_type.54
  22.0 3.9 %collective-permute-done.1 = bf16[2,64,256]{2,1,0:T(8,128)(2,1)S(1)} collective-permute-done((bf16[2,64,256]{2,1,0:T(8,128)(2,1)S(1)}, bf16[2,64,256]{2,1,0:T(8,128)(2,1)S(1)}, u32[]{:S(2)}, u32[]{:S(2)}) %collective-permute-start.1) | collective-permute-done | bytes 65568 | tf_op jit(solution)/shard_map/ppermute | solution.py:25
  25.9 5.1 %all-to-all-start = ((bf16[4,1,4]{2,1,0:T(2,128)(2,1)}), bf16[4,1,4]{2,1,0:T(2,128)(2,1)S(1)}, u32[]{:S(2)}, u32[]{:S(2)}) async-start(bf16[4,1,4]{2,1,0:T(2,128)(2,1)} %convert_element_type.54), calls=%async_computation | async-start | bytes 4096 | tf_op jit(solution)/shard_map/all_to_all | solution.py:222
  31.1 2.0 %copy-done.1 = bf16[27,256,256]{2,1,0:T(8,128)(2,1)S(1)} copy-done((bf16[27,256,256]{2,1,0:T(8,128)(2,1)S(1)}, bf16[27,256,256]{2,1,0:T(8,128)(2,1)}, u32[]{:S(2)}) %copy-start.1) | copy-done | bytes 3538968
  33.1 20.6 %conv.1 = bf16[512,256]{1,0:T(8,128)(2,1)S(1)} custom-call(s32[27,512]{1,0:T(8,128)S(1)} %copy-done.8, bf16[1280,256]{1,0:T(8,128)(2,1)S(1)} %pad_maximum_fusion.pool_ref, bf16[27,256,256]{2,1,0:T(8,128)(2,1)S(1)} %copy-done.1, bf16[512,256]{1,0:T(8,128)(2,1)S(1)} %copy-done.2, bf16[256,256]{1,0:T(8,128)(2,1)S(1)} %copy-done.6, f32[1,256]{1,0:T(1,128)S(1)} %bitcast.24, ...), custom_call_target="tpu_custom_call" | custom-call | tf_op jit(solution)/shard_map/conv/pallas_call | solution.py:86
  53.8 0.4 convolution_convert_fusion
  54.2 1.0 reshape.109
  55.3 5.1 %all-to-all-start.2 = ((bf16[4,4,16384]{2,1,0:T(4,128)(2,1)}), bf16[4,4,16384]{2,1,0:T(4,128)(2,1)S(1)}, u32[]{:S(2)}, u32[]{:S(2)}) async-start(bf16[4,4,16384]{2,1,0:T(4,128)(2,1)} %reshape.109), calls=%async_computation.2 | async-start | bytes 1048576 | tf_op jit(solution)/shard_map/all_to_all | solution.py:221
  60.5 11.8 %all-to-all-done.2 = bf16[4,4,16384]{2,1,0:T(4,128)(2,1)S(1)} async-done(((bf16[4,4,16384]{2,1,0:T(4,128)(2,1)}), bf16[4,4,16384]{2,1,0:T(4,128)(2,1)S(1)}, u32[]{:S(2)}, u32[]{:S(2)}) %all-to-all-start.2) | async-done | bytes 524320 | tf_op jit(solution)/shard_map/all_to_all | solution.py:221
  72.4 0.3 convolution_convert_fusion.1
  73.0 0.2 fusion.3
  73.4 1.1 convolution_convert_fusion.2
  74.8 0.3 fusion.query_ref
  75.1 6.8 %all-gather.5.cloned.1.call-done.pairs_ref = bf16[1024,512]{1,0:T(8,128)(2,1)} async-done(((bf16[512,512]{1,0:T(8,128)(2,1)}), bf16[1024,512]{1,0:T(8,128)(2,1)}) %all-gather.5.cloned.1.call-update) | async-done | bytes 1048592 | tf_op jit(solution)/shard_map/all_gather | solution.py:239
  81.9 1.2 copy-done.3
  83.2 39.4 %tail.1 = bf16[512,256]{1,0:T(8,128)(2,1)} custom-call(bf16[512,256]{1,0:T(8,128)(2,1)S(1)} %reshape.111.rows_ref, bf16[512,256]{1,0:T(8,128)(2,1)S(1)} %fusion.query_ref, bf16[1024,512]{1,0:T(8,128)(2,1)S(1)} %copy-done.3, s32[512,1]{1,0:T(8,128)S(1)} %copy.42.own_ref, s32[1,1024]{1,0:T(1,128)S(1)} %bitcast.22, bf16[256,256]{1,0:T(8,128)(2,1)S(1)} %copy-done.7, ...), custom_call_target="tpu_custom_call" | custom-call | tf_op jit(solution)/shard_map/tail/pallas_call | solution.py:140
  (68 shorter events, 1.6 us)
Async XLA Ops:
  6.5 66.7 %copy-start = (bf16[256,512]{1,0:T(8,128)(2,1)S(1)}, bf16[256,512]{1,0:T(8,128)(2,1)}, u32[]{:S(2)}) copy-start(bf16[256,512]{1,0:T(8,128)(2,1)} %param.33) | copy-start | bytes 786436
  6.5 24.5 %all-gather.3.cloned.1.call-start = ((), (), s32[]{:S(2)}) async-start(), calls=%async_computation.3 | async-start | bytes 5308416 | tf_op jit(solution)/shard_map/all_gather | solution.py:195
  7.3 13.7 %copy-start.19 = (s32[8]{0:T(128)S(1)}, s32[8]{0:T(128)}, u32[]{:S(2)}) copy-start(s32[8]{0:T(128)} %param.23) | copy-start | bytes 100
  9.7 16.1 %all-to-all-start.1 = ((bf16[4,2,64,256]{3,2,1,0:T(8,128)(2,1)}), bf16[4,2,64,256]{3,2,1,0:T(8,128)(2,1)S(1)}, u32[]{:S(2)}, u32[]{:S(2)}) async-start(bf16[4,2,64,256]{3,2,1,0:T(8,128)(2,1)} %select_select_fusion), calls=%async_computation.1 | async-start | bytes 524288 | tf_op jit(solution)/shard_map/all_to_all | solution.py:193
  16.1 15.0 %copy-start.6 = (bf16[256,256]{1,0:T(8,128)(2,1)S(1)}, bf16[256,256]{1,0:T(8,128)(2,1)}, u32[]{:S(2)}) copy-start(bf16[256,256]{1,0:T(8,128)(2,1)} %lin_ref.1) | copy-start | bytes 393220
  16.1 15.0 %copy-start.8 = (s32[27,512]{1,0:T(8,128)S(1)}, s32[27,512]{1,0:T(8,128)}, u32[]{:S(2)}) copy-start(s32[27,512]{1,0:T(8,128)} %nbr_ref.1) | copy-start | bytes 165892
  16.1 15.0 %copy-start.11 = (f32[256]{0:T(256)S(1)}, f32[256]{0:T(256)}, u32[]{:S(2)}) copy-start(f32[256]{0:T(256)} %param.27) | copy-start | bytes 3076
  16.1 15.0 %copy-start.12 = (f32[256]{0:T(256)S(1)}, f32[256]{0:T(256)}, u32[]{:S(2)}) copy-start(f32[256]{0:T(256)} %param.28) | copy-start | bytes 3076
  16.1 15.0 %copy-start.13 = (f32[256]{0:T(256)S(1)}, f32[256]{0:T(256)}, u32[]{:S(2)}) copy-start(f32[256]{0:T(256)} %param.29) | copy-start | bytes 3076
  16.1 5.8 %collective-permute-start = (bf16[2,64,256]{2,1,0:T(8,128)(2,1)S(1)}, bf16[2,64,256]{2,1,0:T(8,128)(2,1)S(1)}, u32[]{:S(2)}, u32[]{:S(2)}) collective-permute-start(bf16[2,64,256]{2,1,0:T(8,128)(2,1)S(1)} %bitcast.33), channel_id=1, source_target_pairs={{0,2},{1,3},{4,6},{5,7},{8,10},{9,11},{12,14},{13,15},{16,18},{17,... | collective-permute-start | bytes 196616 | tf_op jit(solution)/shard_map/ppermute | solution.py:22
  19.7 6.2 %collective-permute-start.1 = (bf16[2,64,256]{2,1,0:T(8,128)(2,1)S(1)}, bf16[2,64,256]{2,1,0:T(8,128)(2,1)S(1)}, u32[]{:S(2)}, u32[]{:S(2)}) collective-permute-start(bf16[2,64,256]{2,1,0:T(8,128)(2,1)S(1)} %bitcast.32), channel_id=1, source_target_pairs={{2,0},{3,1},{6,4},{7,5},{10,8},{11,9},{14,12},{15,13},{18,16},{19,... | collective-permute-start | bytes 196616 | tf_op jit(solution)/shard_map/ppermute | solution.py:25
  25.9 29.4 %all-to-all-start = ((bf16[4,1,4]{2,1,0:T(2,128)(2,1)}), bf16[4,1,4]{2,1,0:T(2,128)(2,1)S(1)}, u32[]{:S(2)}, u32[]{:S(2)}) async-start(bf16[4,1,4]{2,1,0:T(2,128)(2,1)} %convert_element_type.54), calls=%async_computation | async-start | bytes 4096 | tf_op jit(solution)/shard_map/all_to_all | solution.py:222
  31.1 2.0 %copy-start.1 = (bf16[27,256,256]{2,1,0:T(8,128)(2,1)S(1)}, bf16[27,256,256]{2,1,0:T(8,128)(2,1)}, u32[]{:S(2)}) copy-start(bf16[27,256,256]{2,1,0:T(8,128)(2,1)} %all-gather.3.cloned.1.call-done.weight_ref) | copy-start | bytes 10616836
  55.3 17.0 %all-to-all-start.2 = ((bf16[4,4,16384]{2,1,0:T(4,128)(2,1)}), bf16[4,4,16384]{2,1,0:T(4,128)(2,1)S(1)}, u32[]{:S(2)}, u32[]{:S(2)}) async-start(bf16[4,4,16384]{2,1,0:T(4,128)(2,1)} %reshape.109), calls=%async_computation.2 | async-start | bytes 1048576 | tf_op jit(solution)/shard_map/all_to_all | solution.py:221
  60.3 21.6 %all-gather.5.cloned.1.call-start = ((), (), s32[]{:S(2)}) async-start(), calls=%async_computation.4 | async-start | bytes 1572864 | tf_op jit(solution)/shard_map/all_gather | solution.py:239
  60.5 12.8 %copy-start.17 = (f32[256]{0:T(256)S(1)}, f32[256]{0:T(256)}, u32[]{:S(2)}) copy-start(f32[256]{0:T(256)} %param.31) | copy-start | bytes 3076
  60.5 12.8 %copy-start.18 = (f32[256]{0:T(256)S(1)}, f32[256]{0:T(256)}, u32[]{:S(2)}) copy-start(f32[256]{0:T(256)} %param.30) | copy-start | bytes 3076
  72.8 1.9 %copy-start.16 = (bf16[256,256]{1,0:T(8,128)(2,1)S(1)}, bf16[256,256]{1,0:T(8,128)(2,1)}, u32[]{:S(2)}) copy-start(bf16[256,256]{1,0:T(8,128)(2,1)} %param.32) | copy-start | bytes 393220
  73.3 8.6 %copy-start.4 = (bf16[256,1024]{1,0:T(8,128)(2,1)S(1)}, bf16[256,1024]{1,0:T(8,128)(2,1)}, u32[]{:S(2)}) copy-start(bf16[256,1024]{1,0:T(8,128)(2,1)} %fc1_ref.1) | copy-start | bytes 1572868
  73.3 8.6 %copy-start.5 = (bf16[1024,256]{1,0:T(8,128)(2,1)S(1)}, bf16[1024,256]{1,0:T(8,128)(2,1)}, u32[]{:S(2)}) copy-start(bf16[1024,256]{1,0:T(8,128)(2,1)} %fc2_ref.1) | copy-start | bytes 1572868
  73.3 8.6 %copy-start.7 = (bf16[256,256]{1,0:T(8,128)(2,1)S(1)}, bf16[256,256]{1,0:T(8,128)(2,1)}, u32[]{:S(2)}) copy-start(bf16[256,256]{1,0:T(8,128)(2,1)} %proj_ref.1) | copy-start | bytes 393220
  73.3 8.6 %copy-start.10 = (f32[1024]{0:T(1024)S(1)}, f32[1024]{0:T(1024)}, u32[]{:S(2)}) copy-start(f32[1024]{0:T(1024)} %param.38) | copy-start | bytes 12292
  73.3 8.6 %copy-start.14 = (f32[256]{0:T(256)S(1)}, f32[256]{0:T(256)}, u32[]{:S(2)}) copy-start(f32[256]{0:T(256)} %param.35) | copy-start | bytes 3076
  73.3 8.6 %copy-start.15 = (f32[256]{0:T(256)S(1)}, f32[256]{0:T(256)}, u32[]{:S(2)}) copy-start(f32[256]{0:T(256)} %param.36) | copy-start | bytes 3076
  (3 other events, 4.9 us)
Sparse Core Ops, SparseCore 0:
  8.9 14.8 all-gather.2
  74.6 7.2 all-gather.4

commit v2 on v1

v2 whole, which is shorter than its diff:
```python
import functools

import jax
import jax.numpy as jnp
from jax import lax
from jax.experimental import pallas as pl
from jax.experimental.pallas import tpu as pltpu
from jax.sharding import PartitionSpec as P

HEAD_DIM = 16
BLOCK = 64
HALO_B = 2
LANES = 128
VMEM_BYTES = 48 * 1024 * 1024


def layer_norm(values, gain, shift):
    mean = jnp.mean(values, axis=-1, keepdims=True)
    centered = values - mean
    var = jnp.mean(centered * centered, axis=-1, keepdims=True)
    return centered * lax.rsqrt(var + 1e-05) * gain + shift


def dot32(a, b):
    return jnp.dot(a, b, preferred_element_type=jnp.float32)


def front_kernel(
    sizes, table_ref, slot_ref, half_ref, *refs,
):
    sources_hbm, (rows_ref, query_ref, pairs_ref) = refs[:10], refs[10:13]
    (
        codes, marks, acc, held, rest, weight, fetch_out, label_out, label_in, moved_out,
        moved_in, pairs_in, fetch_sem, halo_sem, weight_sem, label_sem, moved_sem, pairs_sem,
        local_sem, load_sem,
    ) = refs[13:33]
    loads = [
        pltpu.make_async_copy(source, held_here, load_sem.at[i])
        for i, (source, held_here) in enumerate(zip(sources_hbm, refs[33:]))
    ]
    for load in loads:
        load.start()
    (
        feat_ref, nbr_ref, lin_ref, bias_ref, gain_ref, shift_ref, gain1_ref, shift1_ref, wq_ref,
        wp_ref,
    ) = refs[33:]
    regions, slabs, chips, slots, cap = sizes
    offsets = weight.shape[0]
    rows, width = feat_ref.shape
    count = rows // BLOCK
    halo = HALO_B * BLOCK
    own_tiles = rows // LANES
    rest_tiles = rest.shape[0] // LANES
    halo_tiles = halo // LANES
    together = 3 if offsets % 3 == 0 else 1
    here, slab, chip = lax.axis_index("region"), lax.axis_index("slab"), lax.axis_index("chip")
    right, left = lax.rem(slab + 1, slabs), lax.rem(slab + slabs - 1, slabs)
    peers = [{"region": lax.rem(here + d, regions)} for d in range(1, regions)]
    mate = {"chip": 1 - chip}

    barrier = pltpu.get_barrier_semaphore()
    for device in peers + [{"slab": right}, {"slab": left}, mate]:
        pl.semaphore_signal(
            barrier, inc=1, device_id=device, device_id_type=pl.DeviceIdType.MESH
        )
    pl.semaphore_wait(barrier, len(peers) + 3)

    def send(src, dst, sems, at, device):
        copy = pltpu.make_async_remote_copy(
            src_ref=src, dst_ref=dst, send_sem=sems.at[0, at], recv_sem=sems.at[1, at],
            device_id=device, device_id_type=pl.DeviceIdType.MESH,
        )
        copy.start()
        return copy

    mine = weight.at[:, :, pl.ds(pl.multiple_of(chip * half_ref.shape[2], LANES), half_ref.shape[2])]
    weight_copy = send(half_ref, mine, weight_sem, 0, mate)
    weight_own = pltpu.make_async_copy(half_ref, mine, local_sem)
    weight_own.start()

    loads[0].wait()

    def chosen(number, ref):
        label = jnp.full((1, width), number.astype(jnp.float32)).astype(jnp.bfloat16)
        block = jnp.zeros((BLOCK, width), jnp.bfloat16)
        for b in range(count):
            block = jnp.where(
                label == jnp.bfloat16(b), ref[b * BLOCK : (b + 1) * BLOCK, :], block
            )
        return block

    fetches = []
    for d in range(regions):
        to = lax.rem(here + d, regions)
        for k in range(slots):
            block = chosen(table_ref[(here * regions + to) * slots + k], feat_ref)
            if d == 0:
                at = 2 * halo + (here * slots + k) * BLOCK
                rest[pl.ds(pl.multiple_of(at, BLOCK), BLOCK), :] = block
            else:
                fetch_out[d - 1, k * BLOCK : (k + 1) * BLOCK, :] = block
        if d > 0:
            at = pl.multiple_of(2 * halo + here * slots * BLOCK, slots * BLOCK)
            fetches.append(
                send(
                    fetch_out.at[d - 1], rest.at[pl.ds(at, slots * BLOCK)], fetch_sem, d - 1,
                    peers[d - 1],
                )
            )
    low = send(
        feat_ref.at[pl.ds(rows - halo, halo)], rest.at[pl.ds(0, halo)], halo_sem, 0,
        {"slab": right},
    )
    high = send(
        feat_ref.at[pl.ds(0, halo)], rest.at[pl.ds(halo, halo)], halo_sem, 1, {"slab": left}
    )

    placed = [slot_ref[b] for b in range(count)]
    region_of = [lax.div(p, count) for p in placed]
    rank = [
        sum([jnp.where(region_of[a] == region_of[b], 1, 0) for a in range(b)], jnp.int32(0))
        for b in range(count)
    ]
    sources = []
    line = lax.broadcasted_iota(jnp.int32, (16, LANES), 0)
    labels = []
    for d in range(regions):
        to = lax.rem(here + d, regions)
        text = jnp.full((16, LANES), -1, jnp.int32)
        source = []
        for k in range(cap):
            block, label = jnp.int32(0), jnp.int32(-1)
            for b in range(count):
                hit = jnp.logical_and(region_of[b] == to, rank[b] == k)
                block = jnp.where(hit, b, block)
                label = jnp.where(hit, lax.rem(placed[b], count), label)
            source.append(block)
            text = jnp.where(line == k, label, text)
        sources.append(source)
        text = text.astype(jnp.float32).astype(jnp.bfloat16)
        if d == 0:
            label_in[0] = text
        else:
            label_out[d - 1] = text
            labels.append(send(label_out.at[d - 1], label_in.at[d], label_sem, d - 1, peers[d - 1]))

    loads[1].wait()
    numbers = nbr_ref[...].T
    low_part = jnp.bitwise_and(numbers, LANES - 1) + LANES
    high_part = jnp.right_shift(jnp.maximum(numbers, 0), 7)
    coded = jnp.where(numbers >= 0, jnp.left_shift(low_part, high_part), 0).astype(jnp.float32)
    for o in range(offsets):
        codes[o] = jnp.broadcast_to(coded[:, o : o + 1], (rows, LANES)).astype(jnp.bfloat16)
    lane = lax.broadcasted_iota(jnp.int32, (16, LANES), 1) + LANES
    for t in range(own_tiles + rest_tiles):
        marks[t] = jnp.left_shift(lane, t).astype(jnp.float32).astype(jnp.bfloat16)
    one = jnp.ones((rows, LANES), jnp.bfloat16)
    zero = jnp.zeros((rows, LANES), jnp.bfloat16)

    def picks(i, tiles):
        lines = []
        for j in range(together):
            code = codes[i * together + j]
            lines.append(
                jnp.concatenate(
                    [
                        jnp.where(code == jnp.tile(marks[t], (rows // 16, 1)), one, zero)
                        for t in tiles
                    ],
                    axis=1,
                )
            )
        return jnp.concatenate(lines, axis=0)

    def own_step(i, carry):
        pick = picks(i, range(halo_tiles, halo_tiles + own_tiles))
        held[i] = dot32(pick, feat_ref[...]).astype(jnp.bfloat16)
        return carry

    lax.fori_loop(0, offsets // together, own_step, 0)
    acc[...] = jnp.zeros_like(acc)
    for copy in fetches + [low, high, weight_copy] + loads[2:]:
        copy.wait()
    weight_own.wait()
    first = rest[0:halo, :]
    rest[0:halo, :] = jnp.where(slab > 0, first, jnp.zeros_like(first))
    second = rest[halo : 2 * halo, :]
    rest[halo : 2 * halo, :] = jnp.where(slab < slabs - 1, second, jnp.zeros_like(second))
    others = list(range(halo_tiles)) + list(
        range(halo_tiles + own_tiles, own_tiles + rest_tiles)
    )

    def rest_step(i, carry):
        got = dot32(picks(i, others), rest[...]).astype(jnp.bfloat16) + held[i]
        total = acc[...]
        for j in range(together):
            total += dot32(got[j * rows : (j + 1) * rows], weight[i * together + j])
        acc[...] = total
        return carry

    lax.fori_loop(0, offsets // together, rest_step, 0)
    conv = acc[...].astype(jnp.bfloat16)
    lin = dot32(conv, lin_ref[...]) + bias_ref[...]
    rows_ref[...] = (
        feat_ref[...].astype(jnp.float32) + layer_norm(lin, gain_ref[...], shift_ref[...])
    ).astype(jnp.bfloat16)

    moves = []
    for d in list(range(1, regions)) + [0]:
        for k in range(cap):
            block = chosen(sources[d][k], rows_ref)
            if d == 0:
                moved_in[0, k * BLOCK : (k + 1) * BLOCK, :] = block
            else:
                moved_out[d - 1, k * BLOCK : (k + 1) * BLOCK, :] = block
        if d > 0:
            moves.append(send(moved_out.at[d - 1], moved_in.at[d], moved_sem, d - 1, peers[d - 1]))
    for copy in labels + moves:
        copy.wait()
    for j in range(count):
        block = jnp.zeros((BLOCK, width), jnp.bfloat16)
        for d in range(regions):
            for k in range(cap):
                label = jnp.tile(label_in[d, k : k + 1, :], (1, width // LANES))
                block = jnp.where(
                    label == jnp.bfloat16(j), moved_in[d, k * BLOCK : (k + 1) * BLOCK, :], block
                )
        rows_ref[j * BLOCK : (j + 1) * BLOCK, :] = block

    normed = layer_norm(
        rows_ref[...].astype(jnp.float32), gain1_ref[...], shift1_ref[...]
    ).astype(jnp.bfloat16)
    ours = pl.ds(pl.multiple_of(chip * rows, rows), rows)
    theirs = pl.ds(pl.multiple_of((1 - chip) * rows, rows), rows)
    pairs = dot32(normed, wp_ref[...]).astype(jnp.bfloat16)
    pairs_in[ours, :] = pairs
    pairs_copy = send(pairs_in.at[ours], pairs_in.at[ours], pairs_sem, 0, mate)
    pairs_ref[ours, :] = pairs
    query = dot32(normed, wq_ref[...]).astype(jnp.bfloat16)
    query_ref[...] = query * jnp.bfloat16(HEAD_DIM ** (-0.5))
    pairs_copy.wait()
    pairs_ref[theirs, :] = pairs_in[theirs, :]


def front_call(
    table, hilbert_slot, neighbours, features, half, lin, bias, gain, shift, gain1, shift1, wq, wp
):
    rows, width = features.shape
    offsets = half.shape[0]
    regions, slabs, chips = (lax.axis_size(axis) for axis in ("region", "slab", "chip"))
    slots = table.shape[2]
    count = rows // BLOCK
    cap = max(1, 2 * count // regions)
    together = 3 if offsets % 3 == 0 else 1
    rest_rows = (2 * HALO_B + regions * slots) * BLOCK
    tiles = (rows + rest_rows) // LANES
    vmem = pl.BlockSpec(memory_space=pltpu.VMEM)
    smem = pl.BlockSpec(memory_space=pltpu.SMEM)
    loaded = [
        features, neighbours, lin, bias[None], gain[None], shift[None], gain1[None],
        shift1[None], wq, wp,
    ]
    shape = jax.ShapeDtypeStruct
    return pl.pallas_call(
        functools.partial(front_kernel, (regions, slabs, chips, slots, cap)),
        out_shape=[
            shape((rows, width), jnp.bfloat16),
            shape((rows, width), jnp.bfloat16),
            shape((chips * rows, 2 * width), jnp.bfloat16),
        ],
        in_specs=[smem, smem] + [pl.BlockSpec(memory_space=pl.ANY)] * (1 + len(loaded)),
        out_specs=[vmem] * 3,
        scratch_shapes=[
            pltpu.VMEM((offsets, rows, LANES), jnp.bfloat16),
            pltpu.VMEM((tiles, 16, LANES), jnp.bfloat16),
            pltpu.VMEM((rows, width), jnp.float32),
            pltpu.VMEM((offsets // together, together * rows, width), jnp.bfloat16),
            pltpu.VMEM((rest_rows, width), jnp.bfloat16),
            pltpu.VMEM((offsets, width, chips * half.shape[2]), jnp.bfloat16),
            pltpu.VMEM((regions - 1, slots * BLOCK, width), jnp.bfloat16),
            pltpu.VMEM((regions - 1, 16, LANES), jnp.bfloat16),
            pltpu.VMEM((regions, 16, LANES), jnp.bfloat16),
            pltpu.VMEM((regions - 1, cap * BLOCK, width), jnp.bfloat16),
            pltpu.VMEM((regions, cap * BLOCK, width), jnp.bfloat16),
            pltpu.VMEM((chips * rows, 2 * width), jnp.bfloat16),
            pltpu.SemaphoreType.DMA((2, regions - 1)),
            pltpu.SemaphoreType.DMA((2, 2)),
            pltpu.SemaphoreType.DMA((2, 1)),
            pltpu.SemaphoreType.DMA((2, regions - 1)),
            pltpu.SemaphoreType.DMA((2, regions - 1)),
            pltpu.SemaphoreType.DMA((2, 1)),
            pltpu.SemaphoreType.DMA,
            pltpu.SemaphoreType.DMA((len(loaded),)),
        ]
        + [pltpu.VMEM(array.shape, array.dtype) for array in loaded],
        compiler_params=pltpu.CompilerParams(
            vmem_limit_bytes=VMEM_BYTES, collective_id=0, has_side_effects=True
        ),
        name="front",
    )(table.reshape(-1), hilbert_slot, half, *loaded)


def tail_kernel(
    rows_ref, query_ref, pairs_ref, ids_ref, proj_ref, gain_ref, shift_ref,
    fc1_ref, fc1_bias_ref, fc2_ref, out_ref, ids, key_marks, own_marks, values, even, odd, mixed,
):
    rows, width = rows_ref.shape
    count = pairs_ref.shape[0]
    heads = width // HEAD_DIM
    zero = jnp.zeros((), jnp.bfloat16)
    lane = lax.broadcasted_iota(jnp.int32, (1, width), 1)
    scan = jnp.bitwise_and(lane, LANES - 1)
    ids[...] = jnp.broadcast_to(ids_ref[...], (LANES, count)).T
    column = jnp.tile(ids[...], (1, width // LANES))
    key_marks[...] = jnp.where(column == scan, 1.0, 0.0).astype(jnp.bfloat16)
    start = pl.multiple_of(lax.axis_index("chip") * rows, rows)
    own = jnp.tile(ids[pl.ds(start, rows), :], (1, width // LANES))
    own_marks[...] = jnp.where(own == scan, 0.0, -1e30).astype(jnp.bfloat16)
    values[...] = pairs_ref[:, width:].T

    def score(h, out):
        mine = lane // HEAD_DIM == h
        query = jnp.where(mine, query_ref[...], own_marks[...])
        keys = jnp.where(mine, pairs_ref[:, :width], key_marks[...])
        out[...] = lax.dot_general(
            keys, query, (((1,), (1,)), ((), ())), preferred_element_type=jnp.float32
        )

    def attend(h, scores):
        held = scores[...]
        top = jnp.max(held, axis=0, keepdims=True)
        expo = jnp.exp(held - top)
        total = jnp.sum(expo, axis=0, keepdims=True)
        weights = (expo * (1.0 / total)).astype(jnp.bfloat16)
        at = pl.ds(pl.multiple_of(h * HEAD_DIM, HEAD_DIM), HEAD_DIM)
        mixed[at, :] = dot32(values[at, :], weights).astype(jnp.bfloat16)

    score(0, even)

    def two_heads(i, carry):
        h = 2 * i
        score(h + 1, odd)
        attend(h, even)
        score(jnp.minimum(h + 2, heads - 1), even)
        attend(h + 1, odd)
        return carry

    lax.fori_loop(0, heads // 2, two_heads, 0)
    attended = mixed[...].T
    mid = (rows_ref[...].astype(jnp.float32) + dot32(attended, proj_ref[...])).astype(jnp.bfloat16)
    mid32 = mid.astype(jnp.float32)
    normed = layer_norm(mid32, gain_ref[...], shift_ref[...]).astype(jnp.bfloat16)
    pre = dot32(normed, fc1_ref[...]) + fc1_bias_ref[...]
    hidden = (0.5 * pre * (1.0 + lax.erf(pre * (0.5**0.5)))).astype(jnp.bfloat16)
    out_ref[...] = (mid32 + dot32(hidden, fc2_ref[...])).astype(jnp.bfloat16)


def tail_call(reordered, queries, pairs, ids, proj, gain, shift, fc1, fc1_bias, fc2):
    rows, width = reordered.shape
    count = pairs.shape[0]
    return pl.pallas_call(
        tail_kernel,
        out_shape=jax.ShapeDtypeStruct((rows, width), jnp.bfloat16),
        in_specs=[pl.BlockSpec(memory_space=pltpu.VMEM)] * 10,
        out_specs=pl.BlockSpec(memory_space=pltpu.VMEM),
        scratch_shapes=[
            pltpu.VMEM((count, LANES), jnp.int32),
            pltpu.VMEM((count, width), jnp.bfloat16),
            pltpu.VMEM((rows, width), jnp.bfloat16),
            pltpu.VMEM((width, count), jnp.bfloat16),
            pltpu.VMEM((count, rows), jnp.float32),
            pltpu.VMEM((count, rows), jnp.float32),
            pltpu.VMEM((width, rows), jnp.bfloat16),
        ],
        compiler_params=pltpu.CompilerParams(vmem_limit_bytes=VMEM_BYTES),
        name="tail",
    )(
        reordered, queries, pairs, ids[None], proj, gain[None], shift[None],
        fc1, fc1_bias[None], fc2,
    )


def local(
    features,
    neighbours,
    fetch_table,
    hilbert_slot,
    patch_ids,
    conv_weight,
    cpe_weight,
    cpe_bias,
    cpe_gain,
    cpe_shift,
    norm1_gain,
    norm1_shift,
    query_weight,
    pair_weight,
    proj_weight,
    norm2_gain,
    norm2_shift,
    fc1_weight,
    fc1_bias,
    fc2_weight,
):
    rows_dev = features.shape[0]
    reordered, query_rows, all_pairs = front_call(
        fetch_table[:, 0, 0], hilbert_slot, neighbours, features, conv_weight, cpe_weight,
        cpe_bias, cpe_gain, cpe_shift, norm1_gain, norm1_shift, query_weight, pair_weight,
    )
    return tail_call(
        reordered, query_rows, all_pairs, patch_ids, proj_weight, norm2_gain,
        norm2_shift, fc1_weight, fc1_bias, fc2_weight,
    )


def solution(mesh):
    return jax.shard_map(
        local,
        mesh=mesh,
        in_specs=(
            P(("groups", "region", "slab", "chip"), None),
            P(None, ("groups", "region", "slab", "chip")),
            P("groups", "slab", "chip", None, None),
            P(("groups", "region", "slab", "chip")),
            P(("groups", "region", "slab")),
            P(None, None, "chip"),
            P(),
            P(),
            P(),
            P(),
            P(),
            P(),
            P(),
            P(),
            P(),
            P(),
            P(),
            P(),
            P(),
            P(),
        ),
        out_specs=P(("groups", "region", "slab", "chip"), None),
        check_vma=False,
    )
```

time: 130 us -> 65 us (0.50)
  waiting for transfers between devices: 23.2 us -> 0 us
  starting transfers between devices: 21.3 us -> 0 us
  between operations: 13.8 us -> 0.09 us
  Pallas kernels: 60 us -> 53.5 us
  local copies, waits for them, and re-layouts: 6.64 us -> 11 us
  other arithmetic: 2.31 us -> 0 us
  matrix products: 2.16 us -> 0 us
    all_to_all x3 -> x0, starting transfers between devices: 16.5 us -> none  [the longest x1 6.32 us: local(): lax.all_to_all(chosen, 'region', split_axis=0, concat_axis=0, tiled=True)]
    all_to_all x3 -> x0, waiting for transfers between devices: 11.8 us -> none  [the longest x1 11.8 us: local(): lax.all_to_all(sending, 'region', split_axis=0, concat_axis=0, tiled=True)]
    unnamed x40 -> x39, local copies, waits for them, and re-layouts: 3.31 us -> 10.9 us
    all_gather x2 -> x0, waiting for transfers between devices: 6.81 us -> none  [the longest x1 6.79 us: local(): all_pairs = lax.all_gather(pair_rows, 'chip', axis=0, tiled=True)]
    pallas_call x2, Pallas kernels: 60 us -> 53.5 us  [the longest x1 37.1 us: front_call(): pl.pallas_call(functools.partial(front_kernel, (regions, slabs, chips, sl...]
    ppermute x2 -> x0, starting transfers between devices: 4.82 us -> none  [the longest x1 3.53 us: with_halo(): lax.ppermute(lax.slice_in_dim(block, block.shape[dim] - width, None, axis...]
    ppermute x2 -> x0, waiting for transfers between devices: 3.86 us -> none  [the longest x1 3.86 us: with_halo(): lax.ppermute(lax.slice_in_dim(block, 0, width, axis=dim), axis, backward)]
    dot_general x4 -> x0, matrix products: 2.16 us -> none  [the longest x1 1.14 us: local(): jnp.dot(normed, pair_weight, preferred_element_type=jnp.float32)]
  transfers between devices with their start and end apart: 7 -> 0, of which waited for: 3 -> 0; matrix products, arithmetic and copies ran while one was open for 4% -> 0% of each run, Pallas kernels for 16% -> 0%
where the time goes in v2:
time: 65 us; the launch traced here: 64.6 us
  Pallas kernels  53.5 us (82%)
  local copies, waits for them, and re-layouts  11 us (17%)
    pallas_call x1, Pallas kernels, front_call(): pl.pallas_call(functools.partial(front_kernel, (regions, slabs, chips, sl...  37.1 us
    pallas_call x1, Pallas kernels, tail_call(): pl.pallas_call(tail_kernel, out_shape=jax.ShapeDtypeStruct((rows, width),...  16.3 us
    unnamed x39, local copies, waits for them, and re-layouts  10.9 us

profile of v2, /device:TPU:0, one launch (start us, length us, event | category | flops | bytes accessed | tf_op | source)
XLA Modules:
  0.0 64.6 jit_solution(2228193549192508546)
XLA Ops:
  0.0 0.8 %copy.22 = s32[4,1,1,4,2]{4,3,0,2,1:T(4,128)S(1)} copy(s32[4,1,1,4,2]{3,4,2,1,0:T(2,128)} %param.22) | data formatting | bytes 256 | tf_op args[2]
  0.9 0.1 reshape_squeeze.3.table_ref
  0.9 0.0 copy-start
  1.0 1.5 %copy-done = bf16[27,256,128]{2,1,0:T(8,128)(2,1)S(1)} copy-done((bf16[27,256,128]{2,1,0:T(8,128)(2,1)S(1)}, bf16[27,256,128]{2,1,0:T(8,128)(2,1)}, u32[]{:S(2)}) %copy-start) | copy-done | bytes 1769496
  2.4 0.9 %copy-done.3 = bf16[512,256]{1,0:T(8,128)(2,1)S(1)} copy-done((bf16[512,256]{1,0:T(8,128)(2,1)S(1)}, bf16[512,256]{1,0:T(8,128)(2,1)}, u32[]{:S(2)}) %copy-start.3) | copy-done | bytes 262168
  3.4 0.9 %copy-done.4 = bf16[256,512]{1,0:T(8,128)(2,1)S(1)} copy-done((bf16[256,512]{1,0:T(8,128)(2,1)S(1)}, bf16[256,512]{1,0:T(8,128)(2,1)}, u32[]{:S(2)}) %copy-start.4) | copy-done | bytes 262168
  4.3 0.9 %copy-done.5 = bf16[256,256]{1,0:T(8,128)(2,1)S(1)} copy-done((bf16[256,256]{1,0:T(8,128)(2,1)S(1)}, bf16[256,256]{1,0:T(8,128)(2,1)}, u32[]{:S(2)}) %copy-start.5) | copy-done | bytes 131096
  5.2 0.9 %copy-done.6 = bf16[256,256]{1,0:T(8,128)(2,1)S(1)} copy-done((bf16[256,256]{1,0:T(8,128)(2,1)S(1)}, bf16[256,256]{1,0:T(8,128)(2,1)}, u32[]{:S(2)}) %copy-start.6) | copy-done | bytes 131096
  6.1 0.8 %copy-done.8 = s32[27,512]{1,0:T(8,128)S(1)} copy-done((s32[27,512]{1,0:T(8,128)S(1)}, s32[27,512]{1,0:T(8,128)}, u32[]{:S(2)}) %copy-start.8) | copy-done | bytes 55320
  7.0 0.7 %copy-done.13 = f32[256]{0:T(256)S(1)} copy-done((f32[256]{0:T(256)S(1)}, f32[256]{0:T(256)}, u32[]{:S(2)}) %copy-start.13) | copy-done | bytes 1048
  7.7 0.7 %copy-done.14 = f32[256]{0:T(256)S(1)} copy-done((f32[256]{0:T(256)S(1)}, f32[256]{0:T(256)}, u32[]{:S(2)}) %copy-start.14) | copy-done | bytes 1048
  8.3 0.7 %copy-done.15 = f32[256]{0:T(256)S(1)} copy-done((f32[256]{0:T(256)S(1)}, f32[256]{0:T(256)}, u32[]{:S(2)}) %copy-start.15) | copy-done | bytes 1048
  9.0 0.7 %copy-done.16 = f32[256]{0:T(256)S(1)} copy-done((f32[256]{0:T(256)S(1)}, f32[256]{0:T(256)}, u32[]{:S(2)}) %copy-start.16) | copy-done | bytes 1048
  9.7 0.7 %copy-done.17 = f32[256]{0:T(256)S(1)} copy-done((f32[256]{0:T(256)S(1)}, f32[256]{0:T(256)}, u32[]{:S(2)}) %copy-start.17) | copy-done | bytes 1048
  10.4 0.7 %copy-done.18 = s32[8]{0:T(128)S(1)} copy-done((s32[8]{0:T(128)S(1)}, s32[8]{0:T(128)}, u32[]{:S(2)}) %copy-start.18) | copy-done | bytes 56
  11.0 37.1 %front.1 = (bf16[512,256]{1,0:T(8,128)(2,1)S(1)}, bf16[512,256]{1,0:T(8,128)(2,1)S(1)}, bf16[1024,512]{1,0:T(8,128)(2,1)S(1)}) custom-call(s32[32]{0:T(128)S(1)} %reshape_squeeze.3.table_ref, s32[8]{0:T(128)S(1)} %copy-done.18, bf16[27,256,128]{2,1,0:T(8,128)(2,1)S(1)} %copy-done, bf16[512,256]{1,0:T(8,128)(2,1)S(1)} %copy-done.3, s32[27,512]{1,0:T(8,128)S(1)} %copy-done.8, ...), custom_call_target="tpu_custom_call" | custom-call | tf_op jit(solution)/shard_map/front/pallas_call | solution.py:264
  48.2 0.0 copy-done.10
  48.2 0.0 copy-done.12
  48.2 0.0 copy-done.11
  48.2 0.0 copy-done.9
  48.2 0.0 copy-done.1
  48.2 0.0 copy-done.2
  48.3 0.0 copy-done.7
  48.3 16.3 %tail.1 = bf16[512,256]{1,0:T(8,128)(2,1)} custom-call(bf16[512,256]{1,0:T(8,128)(2,1)S(1)} %get-tuple-element.8.rows_ref, bf16[512,256]{1,0:T(8,128)(2,1)S(1)} %get-tuple-element.9.query_ref, bf16[1024,512]{1,0:T(8,128)(2,1)S(1)} %get-tuple-element.10.pairs_ref, s32[1,1024]{1,0:T(1,128)S(1)} %bitcast.11, bf16[256,256]{1,0:T(8,128)(2,1)S(1)} %copy-done.7, ...), custom_call_target="tpu_custom_call" | custom-call | tf_op jit(solution)/shard_map/tail/pallas_call | solution.py:361
  (18 shorter events, 0.0 us)
Async XLA Ops:
  0.0 48.2 %copy-start.10 = (f32[1024]{0:T(1024)S(1)}, f32[1024]{0:T(1024)}, u32[]{:S(2)}) copy-start(f32[1024]{0:T(1024)} %param.38) | copy-start | bytes 12292
  0.0 48.2 %copy-start.12 = (f32[256]{0:T(256)S(1)}, f32[256]{0:T(256)}, u32[]{:S(2)}) copy-start(f32[256]{0:T(256)} %param.36) | copy-start | bytes 3076
  0.0 48.2 %copy-start.11 = (f32[256]{0:T(256)S(1)}, f32[256]{0:T(256)}, u32[]{:S(2)}) copy-start(f32[256]{0:T(256)} %param.35) | copy-start | bytes 3076
  0.0 48.2 %copy-start.9 = (s32[1024]{0:T(1024)S(1)}, s32[1024]{0:T(1024)}, u32[]{:S(2)}) copy-start(s32[1024]{0:T(1024)} %param.24) | copy-start | bytes 12292
  0.9 1.5 %copy-start = (bf16[27,256,128]{2,1,0:T(8,128)(2,1)S(1)}, bf16[27,256,128]{2,1,0:T(8,128)(2,1)}, u32[]{:S(2)}) copy-start(bf16[27,256,128]{2,1,0:T(8,128)(2,1)} %half_ref.1) | copy-start | bytes 5308420
  2.4 0.9 %copy-start.3 = (bf16[512,256]{1,0:T(8,128)(2,1)S(1)}, bf16[512,256]{1,0:T(8,128)(2,1)}, u32[]{:S(2)}) copy-start(bf16[512,256]{1,0:T(8,128)(2,1)} %refs_0_.1) | copy-start | bytes 786436
  3.4 0.9 %copy-start.4 = (bf16[256,512]{1,0:T(8,128)(2,1)S(1)}, bf16[256,512]{1,0:T(8,128)(2,1)}, u32[]{:S(2)}) copy-start(bf16[256,512]{1,0:T(8,128)(2,1)} %refs_9_.1) | copy-start | bytes 786436
  4.3 0.9 %copy-start.5 = (bf16[256,256]{1,0:T(8,128)(2,1)S(1)}, bf16[256,256]{1,0:T(8,128)(2,1)}, u32[]{:S(2)}) copy-start(bf16[256,256]{1,0:T(8,128)(2,1)} %refs_2_.1) | copy-start | bytes 393220
  5.2 0.9 %copy-start.6 = (bf16[256,256]{1,0:T(8,128)(2,1)S(1)}, bf16[256,256]{1,0:T(8,128)(2,1)}, u32[]{:S(2)}) copy-start(bf16[256,256]{1,0:T(8,128)(2,1)} %refs_8_.1) | copy-start | bytes 393220
  6.1 0.8 %copy-start.8 = (s32[27,512]{1,0:T(8,128)S(1)}, s32[27,512]{1,0:T(8,128)}, u32[]{:S(2)}) copy-start(s32[27,512]{1,0:T(8,128)} %refs_1_.1) | copy-start | bytes 165892
  7.0 0.7 %copy-start.13 = (f32[256]{0:T(256)S(1)}, f32[256]{0:T(256)}, u32[]{:S(2)}) copy-start(f32[256]{0:T(256)} %param.27) | copy-start | bytes 3076
  7.7 0.7 %copy-start.14 = (f32[256]{0:T(256)S(1)}, f32[256]{0:T(256)}, u32[]{:S(2)}) copy-start(f32[256]{0:T(256)} %param.28) | copy-start | bytes 3076
  8.3 0.7 %copy-start.15 = (f32[256]{0:T(256)S(1)}, f32[256]{0:T(256)}, u32[]{:S(2)}) copy-start(f32[256]{0:T(256)} %param.29) | copy-start | bytes 3076
  9.0 0.7 %copy-start.16 = (f32[256]{0:T(256)S(1)}, f32[256]{0:T(256)}, u32[]{:S(2)}) copy-start(f32[256]{0:T(256)} %param.30) | copy-start | bytes 3076
  9.7 0.7 %copy-start.17 = (f32[256]{0:T(256)S(1)}, f32[256]{0:T(256)}, u32[]{:S(2)}) copy-start(f32[256]{0:T(256)} %param.31) | copy-start | bytes 3076
  10.4 0.7 %copy-start.18 = (s32[8]{0:T(128)S(1)}, s32[8]{0:T(128)}, u32[]{:S(2)}) copy-start(s32[8]{0:T(128)} %slot_ref.1) | copy-start | bytes 100
  11.0 37.2 %copy-start.1 = (bf16[256,1024]{1,0:T(8,128)(2,1)S(1)}, bf16[256,1024]{1,0:T(8,128)(2,1)}, u32[]{:S(2)}) copy-start(bf16[256,1024]{1,0:T(8,128)(2,1)} %fc1_ref.1) | copy-start | bytes 1572868
  11.0 37.2 %copy-start.2 = (bf16[1024,256]{1,0:T(8,128)(2,1)S(1)}, bf16[1024,256]{1,0:T(8,128)(2,1)}, u32[]{:S(2)}) copy-start(bf16[1024,256]{1,0:T(8,128)(2,1)} %fc2_ref.1) | copy-start | bytes 1572868
  11.0 37.2 %copy-start.7 = (bf16[256,256]{1,0:T(8,128)(2,1)S(1)}, bf16[256,256]{1,0:T(8,128)(2,1)}, u32[]{:S(2)}) copy-start(bf16[256,256]{1,0:T(8,128)(2,1)} %proj_ref.1) | copy-start | bytes 393220

commit v3 on v2

--- a/solution.py
+++ b/solution.py
@@ -11,7 +11,7 @@
 BLOCK = 64
 HALO_B = 2
 LANES = 128
-VMEM_BYTES = 48 * 1024 * 1024
+VMEM_BYTES = 64 * 1024 * 1024
 
 
 def layer_norm(values, gain, shift):
@@ -28,22 +28,22 @@
 def front_kernel(
     sizes, table_ref, slot_ref, half_ref, *refs,
 ):
-    sources_hbm, (rows_ref, query_ref, pairs_ref) = refs[:10], refs[10:13]
+    sources_hbm, results = refs[:10], refs[10:13]
     (
         codes, marks, acc, held, rest, weight, fetch_out, label_out, label_in, moved_out,
         moved_in, pairs_in, fetch_sem, halo_sem, weight_sem, label_sem, moved_sem, pairs_sem,
-        local_sem, load_sem,
-    ) = refs[13:33]
+        local_sem, load_sem, rows_ref, query_ref, pairs_ref, save_sem,
+    ) = refs[13:37]
     loads = [
         pltpu.make_async_copy(source, held_here, load_sem.at[i])
-        for i, (source, held_here) in enumerate(zip(sources_hbm, refs[33:]))
+        for i, (source, held_here) in enumerate(zip(sources_hbm, refs[37:]))
     ]
     for load in loads:
         load.start()
     (
         feat_ref, nbr_ref, lin_ref, bias_ref, gain_ref, shift_ref, gain1_ref, shift1_ref, wq_ref,
         wp_ref,
-    ) = refs[33:]
+    ) = refs[37:]
     regions, slabs, chips, slots, cap = sizes
     offsets = weight.shape[0]
     rows, width = feat_ref.shape
@@ -93,7 +93,7 @@
     for d in range(regions):
         to = lax.rem(here + d, regions)
         for k in range(slots):
-            block = chosen(table_ref[(here * regions + to) * slots + k], feat_ref)
+            block = chosen(table_ref[here, 0, 0, to, k], feat_ref)
             if d == 0:
                 at = 2 * halo + (here * slots + k) * BLOCK
                 rest[pl.ds(pl.multiple_of(at, BLOCK), BLOCK), :] = block
@@ -238,8 +238,20 @@
     pairs_ref[ours, :] = pairs
     query = dot32(normed, wq_ref[...]).astype(jnp.bfloat16)
     query_ref[...] = query * jnp.bfloat16(HEAD_DIM ** (-0.5))
+    saves = [
+        pltpu.make_async_copy(rows_ref, results[0], save_sem.at[0]),
+        pltpu.make_async_copy(query_ref, results[1], save_sem.at[1]),
+        pltpu.make_async_copy(pairs_ref.at[ours], results[2].at[ours], save_sem.at[2]),
+    ]
+    for save in saves:
+        save.start()
     pairs_copy.wait()
-    pairs_ref[theirs, :] = pairs_in[theirs, :]
+    saves.append(
+        pltpu.make_async_copy(pairs_in.at[theirs], results[2].at[theirs], save_sem.at[3])
+    )
+    saves[3].start()
+    for save in saves:
+        save.wait()
 
 
 def front_call(
@@ -248,13 +260,12 @@
     rows, width = features.shape
     offsets = half.shape[0]
     regions, slabs, chips = (lax.axis_size(axis) for axis in ("region", "slab", "chip"))
-    slots = table.shape[2]
+    slots = table.shape[4]
     count = rows // BLOCK
     cap = max(1, 2 * count // regions)
     together = 3 if offsets % 3 == 0 else 1
     rest_rows = (2 * HALO_B + regions * slots) * BLOCK
     tiles = (rows + rest_rows) // LANES
-    vmem = pl.BlockSpec(memory_space=pltpu.VMEM)
     smem = pl.BlockSpec(memory_space=pltpu.SMEM)
     loaded = [
         features, neighbours, lin, bias[None], gain[None], shift[None], gain1[None],
@@ -268,8 +279,8 @@
             shape((rows, width), jnp.bfloat16),
             shape((chips * rows, 2 * width), jnp.bfloat16),
         ],
-        in_specs=[smem, smem] + [pl.BlockSpec(memory_space=pl.ANY)] * (1 + len(loaded)),
-        out_specs=[vmem] * 3,
+        in_specs=[smem, smem] + [pl.BlockSpec(memory_space=pltpu.HBM)] * (1 + len(loaded)),
+        out_specs=[pl.BlockSpec(memory_space=pltpu.HBM)] * 3,
         scratch_shapes=[
             pltpu.VMEM((offsets, rows, LANES), jnp.bfloat16),
             pltpu.VMEM((tiles, 16, LANES), jnp.bfloat16),
@@ -291,19 +302,35 @@
             pltpu.SemaphoreType.DMA((2, 1)),
             pltpu.SemaphoreType.DMA,
             pltpu.SemaphoreType.DMA((len(loaded),)),
+            pltpu.VMEM((rows, width), jnp.bfloat16),
+            pltpu.VMEM((rows, width), jnp.bfloat16),
+            pltpu.VMEM((chips * rows, 2 * width), jnp.bfloat16),
+            pltpu.SemaphoreType.DMA((4,)),
         ]
         + [pltpu.VMEM(array.shape, array.dtype) for array in loaded],
         compiler_params=pltpu.CompilerParams(
             vmem_limit_bytes=VMEM_BYTES, collective_id=0, has_side_effects=True
         ),
         name="front",
-    )(table.reshape(-1), hilbert_slot, half, *loaded)
+    )(table, hilbert_slot, half, *loaded)
 
 
 def tail_kernel(
-    rows_ref, query_ref, pairs_ref, ids_ref, proj_ref, gain_ref, shift_ref,
-    fc1_ref, fc1_bias_ref, fc2_ref, out_ref, ids, key_marks, own_marks, values, even, odd, mixed,
+    *refs,
 ):
+    out_ref, ids, key_marks, own_marks, values, even, odd, mixed, load_sem = refs[10:19]
+    loads = [
+        pltpu.make_async_copy(source, held, load_sem.at[i])
+        for i, (source, held) in enumerate(zip(refs[:10], refs[19:]))
+    ]
+    for load in loads:
+        load.start()
+    (
+        pairs_ref, query_ref, ids_ref, rows_ref, proj_ref, gain_ref, shift_ref, fc1_ref,
+        fc1_bias_ref, fc2_ref,
+    ) = refs[19:]
+    for load in loads[:3]:
+        load.wait()
     rows, width = rows_ref.shape
     count = pairs_ref.shape[0]
     heads = width // HEAD_DIM
@@ -346,23 +373,32 @@
         return carry
 
     lax.fori_loop(0, heads // 2, two_heads, 0)
+    for load in loads[3:]:
+        load.wait()
     attended = mixed[...].T
     mid = (rows_ref[...].astype(jnp.float32) + dot32(attended, proj_ref[...])).astype(jnp.bfloat16)
     mid32 = mid.astype(jnp.float32)
     normed = layer_norm(mid32, gain_ref[...], shift_ref[...]).astype(jnp.bfloat16)
     pre = dot32(normed, fc1_ref[...]) + fc1_bias_ref[...]
     hidden = (0.5 * pre * (1.0 + lax.erf(pre * (0.5**0.5)))).astype(jnp.bfloat16)
-    out_ref[...] = (mid32 + dot32(hidden, fc2_ref[...])).astype(jnp.bfloat16)
+    rows_ref[...] = (mid32 + dot32(hidden, fc2_ref[...])).astype(jnp.bfloat16)
+    save = pltpu.make_async_copy(rows_ref, out_ref, load_sem.at[len(loads)])
+    save.start()
+    save.wait()
 
 
 def tail_call(reordered, queries, pairs, ids, proj, gain, shift, fc1, fc1_bias, fc2):
     rows, width = reordered.shape
     count = pairs.shape[0]
+    loaded = [
+        pairs, queries, ids[None], reordered, proj, gain[None], shift[None], fc1, fc1_bias[None],
+        fc2,
+    ]
     return pl.pallas_call(
         tail_kernel,
         out_shape=jax.ShapeDtypeStruct((rows, width), jnp.bfloat16),
-        in_specs=[pl.BlockSpec(memory_space=pltpu.VMEM)] * 10,
-        out_specs=pl.BlockSpec(memory_space=pltpu.VMEM),
+        in_specs=[pl.BlockSpec(memory_space=pltpu.HBM)] * len(loaded),
+        out_specs=pl.BlockSpec(memory_space=pltpu.HBM),
         scratch_shapes=[
             pltpu.VMEM((count, LANES), jnp.int32),
             pltpu.VMEM((count, width), jnp.bfloat16),
@@ -371,13 +407,12 @@
             pltpu.VMEM((count, rows), jnp.float32),
             pltpu.VMEM((count, rows), jnp.float32),
             pltpu.VMEM((width, rows), jnp.bfloat16),
-        ],
+            pltpu.SemaphoreType.DMA((len(loaded) + 1,)),
+        ]
+        + [pltpu.VMEM(array.shape, array.dtype) for array in loaded],
         compiler_params=pltpu.CompilerParams(vmem_limit_bytes=VMEM_BYTES),
         name="tail",
-    )(
-        reordered, queries, pairs, ids[None], proj, gain[None], shift[None],
-        fc1, fc1_bias[None], fc2,
-    )
+    )(*loaded)
 
 
 def local(
@@ -404,7 +439,7 @@
 ):
     rows_dev = features.shape[0]
     reordered, query_rows, all_pairs = front_call(
-        fetch_table[:, 0, 0], hilbert_slot, neighbours, features, conv_weight, cpe_weight,
+        fetch_table, hilbert_slot, neighbours, features, conv_weight, cpe_weight,
         cpe_bias, cpe_gain, cpe_shift, norm1_gain, norm1_shift, query_weight, pair_weight,
     )
     return tail_call(

time: 65 us -> 56.6 us (0.87)
  local copies, waits for them, and re-layouts: 11 us -> 1.38 us
  Pallas kernels: 53.5 us -> 54.9 us
    unnamed x39 -> x1, local copies, waits for them, and re-layouts: 10.9 us -> 1.38 us
    pallas_call x1, Pallas kernels: 16.3 us -> 17.5 us  [tail_call(): pl.pallas_call(tail_kernel, out_shape=jax.ShapeDtypeStruct((rows, width),...]
where the time goes in v3:
time: 56.6 us; the launch traced here: 56.3 us
  Pallas kernels  54.9 us (97%)
  local copies, waits for them, and re-layouts  1.38 us (2%)
    pallas_call x1, Pallas kernels, front_call(): pl.pallas_call(functools.partial(front_kernel, (regions, slabs, chips, sl...  37.5 us
    pallas_call x1, Pallas kernels, tail_call(): pl.pallas_call(tail_kernel, out_shape=jax.ShapeDtypeStruct((rows, width),...  17.5 us
    unnamed x1, local copies, waits for them, and re-layouts  1.38 us

profile of v3, /device:TPU:0, one launch (start us, length us, event | category | flops | bytes accessed | tf_op | source)
XLA Modules:
  0.0 56.3 jit_solution(5528387132248888455)
XLA Ops:
  0.0 1.4 %copy.21.table_ref = s32[4,1,1,4,2]{4,3,2,1,0:T(4,128)} copy(s32[4,1,1,4,2]{3,4,2,1,0:T(2,128)} %param.22) | data formatting | bytes 256 | tf_op args[2]
  1.4 37.5 %front.1 = (bf16[512,256]{1,0:T(8,128)(2,1)}, bf16[512,256]{1,0:T(8,128)(2,1)}, bf16[1024,512]{1,0:T(8,128)(2,1)}) custom-call(s32[4,1,1,4,2]{4,3,2,1,0:T(4,128)} %copy.21.table_ref, s32[8]{0:T(128)} %slot_ref.1, bf16[27,256,128]{2,1,0:T(8,128)(2,1)} %half_ref.1, bf16[512,256]{1,0:T(8,128)(2,1)} %refs_0_.1, s32[27,512]{1,0:T(8,128)} %refs_1_.1, ...), custom_call_target="tpu_custom_call" | custom-call | tf_op jit(solution)/shard_map/front/pallas_call | solution.py:275
  38.8 17.5 %tail.1 = bf16[512,256]{1,0:T(8,128)(2,1)} custom-call(bf16[1024,512]{1,0:T(8,128)(2,1)} %get-tuple-element.8.refs_0_, bf16[512,256]{1,0:T(8,128)(2,1)} %get-tuple-element.9.refs_1_, s32[1,1024]{1,0:T(1,128)} %bitcast.9, bf16[512,256]{1,0:T(8,128)(2,1)} %get-tuple-element.10.refs_3_, bf16[256,256]{1,0:T(8,128)(2,1)} %refs_4_.1, f32[1,256]{1,0:T(1,128)} %bitcast.11, ...), custom_call_target="tpu_custom_call" | custom-call | tf_op jit(solution)/shard_map/tail/pallas_call | solution.py:397

commit v4 on v3

--- a/solution.py
+++ b/solution.py
@@ -329,8 +329,7 @@
         pairs_ref, query_ref, ids_ref, rows_ref, proj_ref, gain_ref, shift_ref, fc1_ref,
         fc1_bias_ref, fc2_ref,
     ) = refs[19:]
-    for load in loads[:3]:
-        load.wait()
+    loads[2].wait()
     rows, width = rows_ref.shape
     count = pairs_ref.shape[0]
     heads = width // HEAD_DIM
@@ -343,6 +342,8 @@
     start = pl.multiple_of(lax.axis_index("chip") * rows, rows)
     own = jnp.tile(ids[pl.ds(start, rows), :], (1, width // LANES))
     own_marks[...] = jnp.where(own == scan, 0.0, -1e30).astype(jnp.bfloat16)
+    for load in loads[:2]:
+        load.wait()
     values[...] = pairs_ref[:, width:].T
 
     def score(h, out):
@@ -358,9 +359,9 @@
         top = jnp.max(held, axis=0, keepdims=True)
         expo = jnp.exp(held - top)
         total = jnp.sum(expo, axis=0, keepdims=True)
-        weights = (expo * (1.0 / total)).astype(jnp.bfloat16)
+        weights = expo.astype(jnp.bfloat16)
         at = pl.ds(pl.multiple_of(h * HEAD_DIM, HEAD_DIM), HEAD_DIM)
-        mixed[at, :] = dot32(values[at, :], weights).astype(jnp.bfloat16)
+        mixed[at, :] = (dot32(values[at, :], weights) * (1.0 / total)).astype(jnp.bfloat16)
 
     score(0, even)
 

time: 56.6 us -> 53.8 us (0.951)
  Pallas kernels: 54.9 us -> 52.2 us
    pallas_call x1, Pallas kernels: 17.5 us -> 14.7 us  [tail_call(): pl.pallas_call(tail_kernel, out_shape=jax.ShapeDtypeStruct((rows, width),...]
where the time goes in v4:
time: 53.8 us; the launch traced here: 53.5 us
  Pallas kernels  52.2 us (97%)
  local copies, waits for them, and re-layouts  1.38 us (3%)
    pallas_call x1, Pallas kernels, front_call(): pl.pallas_call(functools.partial(front_kernel, (regions, slabs, chips, sl...  37.5 us
    pallas_call x1, Pallas kernels, tail_call(): pl.pallas_call(tail_kernel, out_shape=jax.ShapeDtypeStruct((rows, width),...  14.7 us
    unnamed x1, local copies, waits for them, and re-layouts  1.38 us

profile of v4, /device:TPU:0, one launch (start us, length us, event | category | flops | bytes accessed | tf_op | source)
XLA Modules:
  0.0 53.5 jit_solution(3291700506405420360)
XLA Ops:
  0.0 1.4 %copy.21.table_ref = s32[4,1,1,4,2]{4,3,2,1,0:T(4,128)} copy(s32[4,1,1,4,2]{3,4,2,1,0:T(2,128)} %param.22) | data formatting | bytes 256 | tf_op args[2]
  1.4 37.5 %front.1 = (bf16[512,256]{1,0:T(8,128)(2,1)}, bf16[512,256]{1,0:T(8,128)(2,1)}, bf16[1024,512]{1,0:T(8,128)(2,1)}) custom-call(s32[4,1,1,4,2]{4,3,2,1,0:T(4,128)} %copy.21.table_ref, s32[8]{0:T(128)} %slot_ref.1, bf16[27,256,128]{2,1,0:T(8,128)(2,1)} %half_ref.1, bf16[512,256]{1,0:T(8,128)(2,1)} %refs_0_.1, s32[27,512]{1,0:T(8,128)} %refs_1_.1, ...), custom_call_target="tpu_custom_call" | custom-call | tf_op jit(solution)/shard_map/front/pallas_call | solution.py:275
  38.8 14.7 %tail.1 = bf16[512,256]{1,0:T(8,128)(2,1)} custom-call(bf16[1024,512]{1,0:T(8,128)(2,1)} %get-tuple-element.8.refs_0_, bf16[512,256]{1,0:T(8,128)(2,1)} %get-tuple-element.9.refs_1_, s32[1,1024]{1,0:T(1,128)} %bitcast.9, bf16[512,256]{1,0:T(8,128)(2,1)} %get-tuple-element.10.refs_3_, bf16[256,256]{1,0:T(8,128)(2,1)} %refs_4_.1, f32[1,256]{1,0:T(1,128)} %bitcast.11, ...), custom_call_target="tpu_custom_call" | custom-call | tf_op jit(solution)/shard_map/tail/pallas_call | solution.py:398
